TPU v7x, 32 devices: a whole 2x2x4 slice. The times are simulated.
32 devices in a mesh: grp: 2 (over x), dp: 16 (over z, y, core).
Axes of the slice: x: 2, y: 2, z: 4, core: 2. Of those that a mesh axis runs over, the one named last changes fastest.
Arguments:
- tokens: bfloat16 [32768, 768], P(('grp', 'dp')), may hold values from -6 to 6
- cotangent: bfloat16 [32768, 768], P(('grp', 'dp')), may hold values from -6 to 6
- w_query: bfloat16 [768, 768], replicated, may hold values from -0.046875 to 0.046875
- w_key: bfloat16 [768, 768], replicated, may hold values from -0.21875 to 0.21875
- w_value: bfloat16 [768, 768], replicated, may hold values from -0.21875 to 0.21875
- w_attn_out: bfloat16 [768, 768], replicated, may hold values from -0.875 to 0.875
- w_inner: bfloat16 [768, 3072], replicated, may hold values from -0.21875 to 0.21875
- w_outer: bfloat16 [3072, 768], replicated, may hold values from -0.15625 to 0.15625
- gain_attn: float32 [768], replicated, may hold values from 0.1 to 1.9
- gain_ffn: float32 [768], replicated, may hold values from 0.1 to 1.9
- bias_table: float32 [32, 12], replicated, may hold values from -4 to 4
- mem_keys: bfloat16 [128, 1536], replicated, may hold values from -6 to 6
- mem_values: bfloat16 [128, 1536], replicated, may hold values from -6 to 6
- mem_ids: int32 [512, 10], P(('grp', 'dp')), may hold values from 0 to 127, all different within a row
- lengths: int32 [512], P(('grp', 'dp')), may hold values from 8 to 64
- buckets: int32 [64, 64], replicated, may hold values from 0 to 31
Outputs:
- out: bfloat16 [32768, 768], P(('grp', 'dp'))
- grad_tokens: bfloat16 [32768, 768], P(('grp', 'dp'))
- grad_w_query: float32 [768, 768], replicated
- grad_w_key: float32 [768, 768], replicated
- grad_w_value: float32 [768, 768], replicated
- grad_w_attn_out: float32 [768, 768], replicated
- grad_w_inner: float32 [768, 3072], replicated
- grad_w_outer: float32 [3072, 768], replicated
- grad_gain_attn: float32 [768], replicated
- grad_gain_ffn: float32 [768], replicated
- grad_bias_table: float32 [32, 12], replicated
- grad_mem_keys: float32 [128, 1536], replicated
- grad_mem_values: float32 [128, 1536], replicated
Inputs may be any that keep to these rules, and one draw needn't show every extreme that they name: `lengths`: rows of a question at or past its length are padding. `mem_ids`: the 10 entries of a question are distinct; every entry is named by some question.
All inputs are finite; a program needn't handle non-finite values.
Results may differ from a plain program's by a relative error of at most 0.013.
The roundings to bfloat16 on the way count: a program that leaves them out, or rounds other values in their place, can miss the bound.
Values sent between devices are 32-bit elements; how exact they have to be, the bound alone decides.
No kernel may reach another device: no remote copies, remote signals or barrier semaphores. Data moves between devices by JAX's collectives and lax.ppermute only.
A program may use at most 256 MiB of HBM per device.

v0:
```python
import jax
import jax.numpy as jnp
from jax import lax
from jax.sharding import PartitionSpec as P

EPS = 1e-06
NEG = -1000000000.0
F32 = jnp.float32
BF16 = jnp.bfloat16
HIGH = lax.Precision.HIGHEST


def matmul(left, right):
    return jnp.dot(left, right, preferred_element_type=F32)


def left_trans(left, right):
    return lax.dot_general(left, right, (((0,), (0,)), ((), ())), preferred_element_type=F32)


def right_trans(left, right):
    return lax.dot_general(left, right, (((1,), (1,)), ((), ())), preferred_element_type=F32)


def norm_parts(values, gain):
    scale = lax.rsqrt(jnp.mean(values * values, axis=-1, keepdims=True) + EPS)
    base = values * scale
    return (scale, base, (base * gain).astype(BF16))


def norm_back(d_normed, scale, base, gain):
    scaled = d_normed * gain
    grad_gain = jnp.sum(d_normed * base, axis=0)
    grad_in = scale * (scaled - base * jnp.mean(scaled * base, axis=-1, keepdims=True))
    return (grad_gain, grad_in)


def gelu_tanh(values):
    return jax.nn.gelu(values, approximate=True)


def attention_scores(query_heads, key_heads, rel_bias, valid):
    scores = jnp.einsum("qihe,qjhe->qhij", query_heads, key_heads, preferred_element_type=F32)
    scores = scores + rel_bias[None]
    return jnp.where(valid[:, None, None, :], scores, NEG)


def reduce_ffn(grad_inner, grad_outer, grad_gain):
    flat_inner = grad_inner.reshape(-1)
    flat_outer = grad_outer.reshape(-1)
    parts = (
        lax.psum_scatter(flat_inner, "grp", scatter_dimension=0, tiled=True),
        lax.psum_scatter(flat_outer, "grp", scatter_dimension=0, tiled=True),
        lax.psum_scatter(grad_gain, "grp", scatter_dimension=0, tiled=True),
    )
    totals = lax.psum((parts[0], parts[1], parts[2]), "dp")
    whole = (
        lax.all_gather(totals[0], "grp", axis=0, tiled=True),
        lax.all_gather(totals[1], "grp", axis=0, tiled=True),
        lax.all_gather(totals[2], "grp", axis=0, tiled=True),
    )
    gain_total = whole[2]
    return (whole[0].reshape(grad_inner.shape), whole[1].reshape(grad_outer.shape), gain_total)


def reduce_attn(
    grad_query, grad_key, grad_value, grad_out, grad_mkeys, grad_mvalues, grad_gain, grad_bias
):
    flat_query = grad_query.reshape(-1)
    flat_key = grad_key.reshape(-1)
    flat_value = grad_value.reshape(-1)
    flat_out = grad_out.reshape(-1)
    flat_mkeys = grad_mkeys.reshape(-1)
    flat_mvalues = grad_mvalues.reshape(-1)
    flat_bias = grad_bias.reshape(-1)
    parts = (
        lax.psum_scatter(flat_query, "grp", scatter_dimension=0, tiled=True),
        lax.psum_scatter(flat_key, "grp", scatter_dimension=0, tiled=True),
        lax.psum_scatter(flat_value, "grp", scatter_dimension=0, tiled=True),
        lax.psum_scatter(flat_out, "grp", scatter_dimension=0, tiled=True),
        lax.psum_scatter(flat_mkeys, "grp", scatter_dimension=0, tiled=True),
        lax.psum_scatter(flat_mvalues, "grp", scatter_dimension=0, tiled=True),
        lax.psum_scatter(grad_gain, "grp", scatter_dimension=0, tiled=True),
        lax.psum_scatter(flat_bias, "grp", scatter_dimension=0, tiled=True),
    )
    totals = lax.psum(
        (parts[0], parts[1], parts[2], parts[3], parts[4], parts[5], parts[6], parts[7]), "dp"
    )
    whole = (
        lax.all_gather(totals[0], "grp", axis=0, tiled=True),
        lax.all_gather(totals[1], "grp", axis=0, tiled=True),
        lax.all_gather(totals[2], "grp", axis=0, tiled=True),
        lax.all_gather(totals[3], "grp", axis=0, tiled=True),
        lax.all_gather(totals[4], "grp", axis=0, tiled=True),
        lax.all_gather(totals[5], "grp", axis=0, tiled=True),
        lax.all_gather(totals[6], "grp", axis=0, tiled=True),
        lax.all_gather(totals[7], "grp", axis=0, tiled=True),
    )
    gain_total = whole[6]
    bias_total = whole[7]
    return (
        whole[0].reshape(grad_query.shape),
        whole[1].reshape(grad_key.shape),
        whole[2].reshape(grad_value.shape),
        whole[3].reshape(grad_out.shape),
        whole[4].reshape(grad_mkeys.shape),
        whole[5].reshape(grad_mvalues.shape),
        gain_total,
        bias_total.reshape(grad_bias.shape),
    )


def body(
    tokens,
    cotangent,
    w_query,
    w_key,
    w_value,
    w_attn_out,
    w_inner,
    w_outer,
    gain_attn,
    gain_ffn,
    bias_table,
    mem_keys,
    mem_values,
    mem_ids,
    lengths,
    buckets,
):
    question_count = lengths.shape[0]
    row_count = tokens.shape[0]
    seq_len = row_count // question_count
    width = tokens.shape[1]
    head_count = bias_table.shape[1]
    head_size = width // head_count
    bucket_count = bias_table.shape[0]
    entries = mem_keys.shape[0]
    top_count = mem_ids.shape[1]
    prefix_rows = mem_keys.shape[1] // width
    extra = top_count * prefix_rows
    span = seq_len + extra
    inputs = tokens.astype(F32)
    scale1, base1, normed1 = norm_parts(inputs, gain_attn)
    query = matmul(normed1, w_query).astype(BF16)
    key_self = matmul(normed1, w_key).astype(BF16)
    value_self = matmul(normed1, w_value).astype(BF16)
    entry_pick = mem_ids.reshape(-1)[:, None] == jnp.arange(entries, dtype=jnp.int32)[None, :]
    entry_low = entry_pick.astype(BF16)
    mem_key = matmul(entry_low, mem_keys).astype(BF16).reshape(question_count, extra, width)
    mem_value = matmul(entry_low, mem_values).astype(BF16).reshape(question_count, extra, width)
    key_heads = jnp.concatenate(
        [key_self.reshape(question_count, seq_len, width), mem_key], axis=1
    ).reshape(question_count, span, head_count, head_size)
    value_heads = jnp.concatenate(
        [value_self.reshape(question_count, seq_len, width), mem_value], axis=1
    ).reshape(question_count, span, head_count, head_size)
    query_heads = query.reshape(question_count, seq_len, head_count, head_size)
    bucket_pick = (
        buckets.reshape(-1)[:, None] == jnp.arange(bucket_count, dtype=jnp.int32)[None, :]
    ).astype(F32)
    bias_rows = jnp.dot(bucket_pick, bias_table, precision=HIGH)
    rel_bias = jnp.transpose(bias_rows.reshape(seq_len, seq_len, head_count), (2, 0, 1))
    rel_bias = jnp.concatenate([rel_bias, jnp.zeros((head_count, seq_len, extra), F32)], axis=2)
    places = jnp.arange(span, dtype=jnp.int32)
    valid = (places[None, :] < lengths[:, None]) | (places[None, :] >= seq_len)
    masked = attention_scores(query_heads, key_heads, rel_bias, valid)
    top = jnp.max(masked, axis=-1, keepdims=True)
    expd = jnp.exp(masked - top)
    denom = jnp.sum(expd, axis=-1, keepdims=True)
    log_total = top + jnp.log(denom)
    probs_low = (expd / denom).astype(BF16)
    attended = (
        jnp.einsum("qhij,qjhe->qihe", probs_low, value_heads, preferred_element_type=F32)
        .astype(BF16)
        .reshape(row_count, width)
    )
    hidden = inputs + matmul(attended, w_attn_out)
    scale2, base2, normed2 = norm_parts(hidden, gain_ffn)
    inner = matmul(normed2, w_inner)
    act_full, gelu_pull = jax.vjp(gelu_tanh, inner)
    act = act_full.astype(BF16)
    out = (hidden + matmul(act, w_outer)).astype(BF16)
    grad_w_outer = left_trans(act, cotangent)
    d_act = right_trans(cotangent, w_outer)
    d_inner = gelu_pull(d_act)[0].astype(BF16)
    grad_w_inner = left_trans(normed2, d_inner)
    d_normed2 = right_trans(d_inner, w_inner)
    grad_gain_ffn, d_hidden_norm = norm_back(d_normed2, scale2, base2, gain_ffn)
    d_hidden = cotangent.astype(F32) + d_hidden_norm
    grad_w_inner, grad_w_outer, grad_gain_ffn = reduce_ffn(
        grad_w_inner, grad_w_outer, grad_gain_ffn
    )
    d_hidden_low = d_hidden.astype(BF16)
    grad_w_attn_out = left_trans(attended, d_hidden_low)
    d_attended = (
        right_trans(d_hidden_low, w_attn_out)
        .astype(BF16)
        .reshape(question_count, seq_len, head_count, head_size)
    )
    masked_again = attention_scores(query_heads, key_heads, rel_bias, valid)
    probs = jnp.exp(masked_again - log_total)
    probs_again = probs.astype(BF16)
    d_values = jnp.einsum("qhij,qihe->qjhe", probs_again, d_attended, preferred_element_type=F32)
    d_probs = jnp.einsum("qihe,qjhe->qhij", d_attended, value_heads, preferred_element_type=F32)
    d_scores = (probs * (d_probs - jnp.sum(probs * d_probs, axis=-1, keepdims=True))).astype(BF16)
    d_query = (
        jnp.einsum("qhij,qjhe->qihe", d_scores, key_heads, preferred_element_type=F32)
        .astype(BF16)
        .reshape(row_count, width)
    )
    d_keys = jnp.einsum("qhij,qihe->qjhe", d_scores, query_heads, preferred_element_type=F32)
    bias_terms = jnp.sum(d_scores[:, :, :, :seq_len].astype(F32), axis=0).reshape(
        head_count, seq_len * seq_len
    )
    grad_bias_table = jnp.transpose(jnp.dot(bias_terms, bucket_pick, precision=HIGH))
    entry_float = entry_pick.astype(F32)
    d_mem_key = d_keys[:, seq_len:].reshape(question_count * top_count, prefix_rows * width)
    d_mem_value = d_values[:, seq_len:].reshape(question_count * top_count, prefix_rows * width)
    grad_mem_keys = lax.dot_general(
        entry_float, d_mem_key, (((0,), (0,)), ((), ())), precision=HIGH
    )
    grad_mem_values = lax.dot_general(
        entry_float, d_mem_value, (((0,), (0,)), ((), ())), precision=HIGH
    )
    d_key_self = d_keys[:, :seq_len].reshape(row_count, width).astype(BF16)
    d_value_self = d_values[:, :seq_len].reshape(row_count, width).astype(BF16)
    grad_w_query = left_trans(normed1, d_query)
    grad_w_key = left_trans(normed1, d_key_self)
    grad_w_value = left_trans(normed1, d_value_self)
    d_normed1 = (
        right_trans(d_query, w_query)
        + right_trans(d_key_self, w_key)
        + right_trans(d_value_self, w_value)
    )
    grad_gain_attn, d_input_norm = norm_back(d_normed1, scale1, base1, gain_attn)
    grad_tokens = (d_hidden + d_input_norm).astype(BF16)
    (
        grad_w_query,
        grad_w_key,
        grad_w_value,
        grad_w_attn_out,
        grad_mem_keys,
        grad_mem_values,
        grad_gain_attn,
        grad_bias_table,
    ) = reduce_attn(
        grad_w_query,
        grad_w_key,
        grad_w_value,
        grad_w_attn_out,
        grad_mem_keys,
        grad_mem_values,
        grad_gain_attn,
        grad_bias_table,
    )
    return (
        out,
        grad_tokens,
        grad_w_query,
        grad_w_key,
        grad_w_value,
        grad_w_attn_out,
        grad_w_inner,
        grad_w_outer,
        grad_gain_attn,
        grad_gain_ffn,
        grad_bias_table,
        grad_mem_keys,
        grad_mem_values,
    )


def solution(mesh):
    placed = (
        P(("grp", "dp"), None),
        P(("grp", "dp"), None),
        P(),
        P(),
        P(),
        P(),
        P(),
        P(),
        P(),
        P(),
        P(),
        P(),
        P(),
        P(("grp", "dp"), None),
        P(("grp", "dp")),
        P(),
    )
    return jax.shard_map(
        body,
        mesh=mesh,
        in_specs=placed,
        out_specs=(
            P(("grp", "dp"), None),
            P(("grp", "dp"), None),
            P(),
            P(),
            P(),
            P(),
            P(),
            P(),
            P(),
            P(),
            P(),
            P(),
            P(),
        ),
        check_vma=False,
    )
```

profile of v0, /device:TPU:0, one launch (start us, length us, event | category | flops | bytes accessed | tf_op | source)
XLA Modules:
  0.0 1713.4 jit_solution(3049151020609751570)
XLA Ops:
  31.8 4.6 copy.114
  36.4 4.5 copy.110
  40.9 5.9 reshape.231
  46.8 6.5 copy.109
  53.3 5.9 reshape.246
  59.2 6.5 copy.123
  65.7 5.9 reshape.232
  71.6 6.7 copy.113
  78.4 8.0 fusion.59
  91.5 6.5 convert_bitcast_fusion.1
  102.2 5.4 reshape.198
  111.0 8.8 fusion.47
  119.8 9.1 fusion.48
  128.9 14.8 fusion.6
  143.7 9.6 multiply_reduce_fusion.1
  153.4 7.6 convolution_bitcast_fusion
  170.6 6.6 copy.127
  177.2 12.0 multiply_reduce_fusion
  196.3 7.5 convert_bitcast_fusion
  207.2 4.3 slice.25
  214.0 4.4 slice.26
  218.4 10.9 reshape.211
  229.4 9.8 copy.151
  240.7 6.0 copy.122
  246.7 5.5 reshape.200
  259.7 6.1 copy.132
  271.5 6.0 copy.124
  277.5 5.8 convert_element_type.100
  283.3 4.3 fusion.51
  290.8 6.1 copy.133
  302.6 6.0 copy.128
  308.6 5.4 convert_element_type.102
  324.6 668.5 %all-reduce.22.cloned.1.call-done = (f32[589824]{0:T(1024)}, f32[589824]{0:T(1024)}, f32[589824]{0:T(1024)}, f32[589824]{0:T(1024)}, f32[2359296]{0:T(1024)}, /*...) async-done(((f32[589824]{0:T(1024)}, f32[589824]{0:T(1024)}, f32[589824]{0:T(1024)}, f32[589824]{0:T(1024)}, f32[2359296]{0:T(1024)}, /*index=5*/f32[2359296]{0:T(1024)}, ...) | async-done | bytes 29884432
  1014.8 273.8 %all-reduce.20.cloned.1.call-done = (f32[294912]{0:T(1024)}, f32[294912]{0:T(1024)}, f32[294912]{0:T(1024)}, f32[294912]{0:T(1024)}, f32[1179648]{0:T(1024)}, /*...) async-done(((f32[294912]{0:T(1024)}, f32[294912]{0:T(1024)}, f32[294912]{0:T(1024)}, f32[294912]{0:T(1024)}, f32[1179648]{0:T(1024)}, /*index=5*/f32[1179648]{0:T(1024)}, ...) | async-done | bytes 14942224 | tf_op jit(solution)/shard_map/psum | solution.py:86
  1293.2 12.5 add_convert_fusion
  1319.8 8.0 all-reduce.15
  1328.1 31.5 %all-reduce.13 = (f32[384]{0:T(512)S(1)}, f32[384]{0:T(512)S(1)}, f32[192]{0:T(256)S(1)}) all-reduce(f32[384]{0:T(512)S(1)} %dynamic-slice.14, f32[384]{0:T(512)S(1)} %dynamic-slice.16, f32[192]{0:T(256)S(1)} %dynamic-slice.18), channel_id=1, replica_groups=mesh['grp'=2,'dp'=16] {'dp'}, use_global_device_ids=true, to_apply=%region_21.22 | all-reduce | flops 960 | bytes 7680 | tf_op jit(solution)/shard_map/psum | solution.py:86
  1359.5 4.3 all-gather
  1364.5 4.3 all-gather.1
  1369.5 5.1 fusion.18
  1378.2 5.0 all-reduce.1
  1384.0 19.6 %all_gather.42 = f32[196608]{0:T(1024)S(1)} all-gather(f32[98304]{0:T(1024)S(1)} %copy-done.22), channel_id=1, replica_groups=mesh['grp'=2,'dp'=16] {'grp'}, dimensions={0}, use_global_device_ids=true | all-gather | bytes 1179648 | tf_op jit(solution)/shard_map/all_gather | solution.py:94
  1404.5 13.8 all_gather.43
  1429.6 26.3 %all-gather.15.cloned.1.call-done = f32[589824]{0:T(1024)} async-done(((f32[294912]{0:T(1024)}), f32[589824]{0:T(1024)}) %all-gather.15.cloned.1.call-update) | async-done | bytes 2359312 | tf_op jit(solution)/shard_map/all_gather | solution.py:93
  1459.3 116.2 %all-gather.17.cloned.1.call-done = f32[2359296]{0:T(1024)} async-done(((f32[1179648]{0:T(1024)}), f32[2359296]{0:T(1024)}) %all-gather.17.cloned.1.call-update) | async-done | bytes 9437200 | tf_op jit(solution)/shard_map/all_gather | solution.py:58
  1575.5 11.0 reshape.210
  1586.6 108.6 %all-gather.19.cloned.1.call-done = f32[2359296]{0:T(1024)} async-done(((f32[1179648]{0:T(1024)}), f32[2359296]{0:T(1024)}) %all-gather.19.cloned.1.call-update) | async-done | bytes 9437200 | tf_op jit(solution)/shard_map/all_gather | solution.py:59
  1695.1 11.3 reshape.212
  (183 shorter events, 151.9 us)
Async XLA Ops:
  7.2 19.4 %copy-start = (bf16[768,768]{1,0:T(8,128)(2,1)S(1)}, bf16[768,768]{1,0:T(8,128)(2,1)}, u32[]{:S(2)}) copy-start(bf16[768,768]{1,0:T(8,128)(2,1)} %param.20) | copy-start | bytes 3538948
  7.2 985.9 %all-reduce.22.cloned.1.call-start = ((), (), s32[]{:S(2)}) async-start(), calls=%async_computation.7 | async-start | bytes 59768832
  8.1 6.8 copy-start.28
  9.0 1.0 copy-start.24
  14.9 4.7 copy-start.30
  19.3 88.3 %copy-start.5 = (bf16[1024,768]{0,1:T(8,128)(2,1)}, bf16[1024,768]{0,1:T(8,128)(2,1)S(1)}, u32[]{:S(2)}) copy-start(bf16[1024,768]{0,1:T(8,128)(2,1)S(1)} %copy.107) | copy-start | bytes 4718596
  19.7 6.9 copy-start.26
  19.7 4.1 copy-start.35
  71.6 6.7 copy-start.33
  86.4 3.8 copy-start.1
  86.4 4.2 copy-start.11
  86.4 5.1 copy-start.12
  107.6 3.4 copy-start.23
  111.0 50.0 %copy-start.10 = (f32[1024,768]{0,1:T(8,128)}, f32[1024,768]{0,1:T(8,128)S(1)}, u32[]{:S(2)}) copy-start(f32[1024,768]{0,1:T(8,128)S(1)} %get-tuple-element.96) | copy-start | bytes 9437188
  111.0 8.8 copy-start.18
  119.8 9.1 copy-start.8
  143.7 9.6 copy-start.37
  153.4 7.6 copy-start.13
  161.0 1.4 copy-start.20
  162.4 2.8 copy-start.9
  162.4 2.8 copy-start.34
  170.6 18.6 %slice-start = ((s8[6291456]{0:T(1024)(128)(4,1)}), s8[2097152]{0:T(1024)(128)(4,1)S(1)}, s32[]{:S(2)}) async-start(s8[6291456]{0:T(1024)(128)(4,1)} %bitcast.68), calls=%async_computation.8 | async-start | bytes 4194304
  177.2 12.0 slice-start.1
  177.2 12.0 copy-start.4
  189.2 3.0 copy-start.7
  196.3 7.5 copy-start.2
  196.3 7.5 copy-start.3
  229.4 9.8 copy-start.17
  246.6 5.5 copy-start.6
  246.6 5.5 copy-start.27
  246.7 5.5 copy-start.31
  265.8 3.0 copy-start.29
  321.5 0.7 copy-start.32
  321.5 967.1 %all-reduce.20.cloned.1.call-start = ((), (), s32[]{:S(2)}) async-start(), calls=%async_computation.6 | async-start | bytes 29884416 | tf_op jit(solution)/shard_map/psum | solution.py:86
  996.7 10.3 copy-start.16
  1007.0 5.4 copy-start.15
  1014.7 404.6 %all-gather.9.cloned.1.call-start = ((), (), s32[]{:S(2)}) async-start(), calls=%async_computation | async-start | bytes 3538944 | tf_op jit(solution)/shard_map/all_gather | solution.py:90
  1288.6 134.1 %all-gather.11.cloned.1.call-start = ((), (), s32[]{:S(2)}) async-start(), calls=%async_computation.1 | async-start | bytes 3538944 | tf_op jit(solution)/shard_map/all_gather | solution.py:91
  1289.2 136.9 %all-gather.13.cloned.1.call-start = ((), (), s32[]{:S(2)}) async-start(), calls=%async_computation.2 | async-start | bytes 3538944 | tf_op jit(solution)/shard_map/all_gather | solution.py:92
  1289.8 166.2 %all-gather.15.cloned.1.call-start = ((), (), s32[]{:S(2)}) async-start(), calls=%async_computation.3 | async-start | bytes 3538944 | tf_op jit(solution)/shard_map/all_gather | solution.py:93
  1290.4 285.2 %all-gather.17.cloned.1.call-start = ((), (), s32[]{:S(2)}) async-start(), calls=%async_computation.4 | async-start | bytes 14155776 | tf_op jit(solution)/shard_map/all_gather | solution.py:58
  1291.1 404.0 %all-gather.19.cloned.1.call-start = ((), (), s32[]{:S(2)}) async-start(), calls=%async_computation.5 | async-start | bytes 14155776 | tf_op jit(solution)/shard_map/all_gather | solution.py:59
  1305.7 5.3 copy-start.25
  1311.5 3.3 copy-start.19
  1311.5 3.3 copy-start.36
  1314.9 1.4 copy-start.14
  1374.5 9.5 copy-start.22
  1374.5 30.0 %copy-start.21 = (f32[98304]{0:T(1024)S(1)}, f32[98304]{0:T(1024)}, u32[]{:S(2)}) copy-start(f32[98304]{0:T(1024)} %get-tuple-element.79) | copy-start | bytes 1179652
Sparse Core Ops, SparseCore 0:
  321.6 671.4 all-reduce.21
  1014.9 273.7 all-reduce.19
  1290.2 36.4 all-gather.8
  1328.0 36.0 all-gather.10
  1365.5 50.3 all-gather.12
  1417.3 38.6 all-gather.14
  1457.5 117.9 all-gather.16
  1577.1 117.9 all-gather.18
where the time goes:
time: 1720 us; the launch traced here: 1710 us
  waiting for transfers between devices  1200 us (70%)
  local copies, waits for them, and re-layouts  248 us (14%)
  matrix products  146 us (8%)
  blocking collectives  86.5 us (5%)
  between operations  18.8 us (1%)
    unnamed x9, waiting for transfers between devices  672 us
    psum x1, waiting for transfers between devices, reduce_attn(): lax.psum((parts[0], parts[1], parts[2], parts[3], parts[4], parts[5], par...  274 us
    all_gather x1, waiting for transfers between devices, reduce_ffn(): lax.all_gather(totals[0], 'grp', axis=0, tiled=True)  116 us
    all_gather x1, waiting for transfers between devices, reduce_ffn(): lax.all_gather(totals[1], 'grp', axis=0, tiled=True)  109 us
    unnamed x104, local copies, waits for them, and re-layouts  47 us
    dot_general x8, matrix products, matmul(): return jnp.dot(left, right, preferred_element_type=F32)  36.8 us
  transfers between devices with their start and end apart: 8, of which 5 were waited for; matrix products, arithmetic and copies ran while one was open for 4% of the time, Pallas kernels for 0%

commit v1 on v0

v1 whole, which is shorter than its diff:
```python
import functools

import jax
import jax.numpy as jnp
from jax import lax
from jax.experimental import pallas as pl
from jax.experimental.pallas import tpu as pltpu
from jax.sharding import PartitionSpec as P

EPS = 1e-06
NEG = -1000000000.0
F32 = jnp.float32
BF16 = jnp.bfloat16
GELU_C = 0.7978845608028654
GELU_A = 0.044715
SMALL = 64
VMEM_LIMIT = 60 * 1024 * 1024
VMEM = pl.BlockSpec(memory_space=pltpu.VMEM)
SMEM = pl.BlockSpec(memory_space=pltpu.SMEM)
ANY = pl.BlockSpec(memory_space=pl.ANY)
COST = pl.CostEstimate(flops=1, bytes_accessed=1, transcendentals=0)


def nn(left, right):
    return lax.dot_general(left, right, (((1,), (0,)), ((), ())), preferred_element_type=F32)


def nt(left, right):
    return lax.dot_general(left, right, (((1,), (1,)), ((), ())), preferred_element_type=F32)


def tn(left, right):
    return lax.dot_general(left, right, (((0,), (0,)), ((), ())), preferred_element_type=F32)


def params():
    return pltpu.CompilerParams(vmem_limit_bytes=VMEM_LIMIT)


def shape(dims, dtype):
    return jax.ShapeDtypeStruct(dims, dtype)


class Sizes:
    def __init__(self, rows, width, questions, heads, buckets, entries, top, mem_width):
        self.rows = rows
        self.width = width
        self.questions = questions
        self.heads = heads
        self.buckets = buckets
        self.entries = entries
        self.top = top
        self.prefix = mem_width // width
        self.seq = rows // questions
        self.dh = width // heads
        self.pad = -(-top // 16) * 16
        self.span = self.seq + self.prefix * self.pad
        self.quad = 4
        self.qw = self.quad * self.dh
        self.quads = heads // self.quad


def head_mask(sz):
    n = sz.quad * sz.seq
    head = lax.broadcasted_iota(jnp.int32, (n, sz.qw), 0) // sz.seq
    lane = lax.broadcasted_iota(jnp.int32, (n, sz.qw), 1) // sz.dh
    return jnp.where(head == lane, 1.0, 0.0).astype(BF16)


def spread(block, mask, sz):
    return jnp.concatenate([block] * sz.quad, axis=0) * mask


def gather_diag(full, sz):
    s = sz.seq
    lane = lax.broadcasted_iota(jnp.int32, (s, 2 * sz.dh), 1)
    parts = []
    for pair in range(sz.quad // 2):
        cols = slice(pair * 2 * sz.dh, (pair + 1) * 2 * sz.dh)
        low = full[(2 * pair) * s : (2 * pair + 1) * s, cols]
        high = full[(2 * pair + 1) * s : (2 * pair + 2) * s, cols]
        parts.append(jnp.where(lane < sz.dh, low, high))
    return jnp.concatenate(parts, axis=1)


def bucket_lanes(buckets_ref, sz):
    row = lax.broadcasted_iota(jnp.int32, (sz.seq, 2 * sz.seq), 0)
    lane = lax.broadcasted_iota(jnp.int32, (sz.seq, 2 * sz.seq), 1)
    pick = jnp.where(lane % sz.seq == row, 1.0, 0.0).astype(BF16)
    return tn(buckets_ref[...].astype(F32).astype(BF16), pick)


def fill_bias(bias_ref, table_ref, buckets_ref, sz):
    bt = bucket_lanes(buckets_ref, sz)
    width = sz.heads * sz.seq
    head = lax.broadcasted_iota(jnp.int32, (sz.heads, width), 0)
    lane = lax.broadcasted_iota(jnp.int32, (sz.heads, width), 1) // sz.seq
    wide = jnp.dot(
        table_ref[...], jnp.where(head == lane, 1.0, 0.0),
        precision=lax.Precision.HIGHEST, preferred_element_type=F32,
    )
    for pair in range(sz.heads // 2):
        cols = slice(pair * 2 * sz.seq, (pair + 1) * 2 * sz.seq)
        acc = jnp.zeros((sz.seq, 2 * sz.seq), F32)
        for b in range(sz.buckets):
            acc = jnp.where(bt == float(b), wide[b : b + 1, cols], acc)
        bias_ref[0 : sz.seq, cols] = acc
    n = sz.prefix * sz.pad
    row = lax.broadcasted_iota(jnp.int32, (n, sz.heads * sz.seq), 0) % sz.pad
    bias_ref[sz.seq :, :] = jnp.where(row < sz.top, 0.0, NEG)


def fill_memory(pick, table_ref, out_ref):
    out_ref[...] = nn(pick, table_ref[...]).astype(BF16)


def one_hot(ids_ref, sz):
    n = sz.questions * sz.pad
    row = lax.broadcasted_iota(jnp.int32, (n, sz.questions), 0) // sz.pad
    question = lax.broadcasted_iota(jnp.int32, (n, sz.questions), 1)
    repeat = jnp.where(row == question, 1.0, 0.0).astype(BF16)
    spread_ids = nn(repeat, (ids_ref[...] + 1).astype(F32).astype(BF16))
    slot = lax.broadcasted_iota(jnp.int32, (n, sz.top), 0) % sz.pad
    own = slot == lax.broadcasted_iota(jnp.int32, (n, sz.top), 1)
    column = jnp.sum(jnp.where(own, spread_ids, 0.0), axis=1, keepdims=True)
    lane = lax.broadcasted_iota(jnp.int32, (n, sz.entries), 1).astype(F32)
    return jnp.where(lane + 1.0 == column, 1.0, 0.0).astype(BF16)


def key_block(self_ref, mem_ref, q, col, sz):
    rows = pl.ds(pl.multiple_of(q * sz.seq, sz.seq), sz.seq)
    mrows = pl.ds(pl.multiple_of(q * sz.pad, sz.pad), sz.pad)
    parts = [self_ref[rows, col : col + sz.qw]]
    for p in range(sz.prefix):
        parts.append(mem_ref[mrows, p * sz.width + col : p * sz.width + col + sz.qw])
    return jnp.concatenate(parts, axis=0)


def probabilities(keys, spread_query, bias, length, sz):
    scores = nt(keys, spread_query) + bias
    row = lax.broadcasted_iota(jnp.int32, scores.shape, 0)
    admitted = jnp.logical_or(row < length, row >= sz.seq)
    scores = jnp.where(admitted, scores, NEG)
    top = jnp.max(scores, axis=0, keepdims=True)
    expd = jnp.exp(scores - top)
    return expd * (1.0 / jnp.sum(expd, axis=0, keepdims=True))


def forward_kernel(
    sz,
    tokens, wq, wk, wv, wo, gain1, gain2, table, mkeys, mvalues, ids, lengths, buckets,
    normed1, query, key, value, attended, hidden, normed2,
    bias, memk, memv,
):
    block = 256
    pick = one_hot(ids, sz)
    fill_memory(pick, mkeys, memk)
    fill_memory(pick, mvalues, memv)
    fill_bias(bias, table, buckets, sz)
    for r in range(0, sz.rows, block):
        x = tokens[r : r + block, :].astype(F32)
        scale = lax.rsqrt(jnp.mean(x * x, axis=-1, keepdims=True) + EPS)
        low = (x * scale * gain1[...].reshape(1, -1)).astype(BF16)
        normed1[r : r + block, :] = low
    for w, out in ((wq, query), (wk, key), (wv, value)):
        for r in range(0, sz.rows, block):
            out[r : r + block, :] = nn(normed1[r : r + block, :], w[...]).astype(BF16)
    mask = head_mask(sz)

    def step(q, carry):
        length = lengths[q]
        rows = pl.ds(pl.multiple_of(q * sz.seq, sz.seq), sz.seq)
        for c in range(sz.quads):
            col = c * sz.qw
            sq = spread(query[rows, col : col + sz.qw], mask, sz)
            keys = key_block(key, memk, q, col, sz)
            values = key_block(value, memv, q, col, sz)
            probs = probabilities(keys, sq, bias[:, col : col + sz.qw], length, sz)
            full = tn(probs.astype(BF16), values)
            attended[rows, col : col + sz.qw] = gather_diag(full, sz).astype(BF16)
        return carry

    lax.fori_loop(0, sz.questions, step, 0)
    for r in range(0, sz.rows, block):
        rows = slice(r, r + block)
        h = tokens[rows, :].astype(F32) + nn(attended[rows, :], wo[...])
        hidden[rows, :] = h
        scale = lax.rsqrt(jnp.mean(h * h, axis=-1, keepdims=True) + EPS)
        normed2[rows, :] = (h * scale * gain2[...].reshape(1, -1)).astype(BF16)


def forward(sz, tokens, wq, wk, wv, wo, gain1, gain2, table, mkeys, mvalues, ids, lengths, buckets):
    n, d = sz.rows, sz.width
    low = shape((n, d), BF16)
    return pl.pallas_call(
        functools.partial(forward_kernel, sz),
        in_specs=[VMEM] * 11 + [SMEM, VMEM],
        out_specs=[VMEM] * 7,
        out_shape=[low, low, low, low, low, shape((n, d), F32), low],
        scratch_shapes=[
            pltpu.VMEM((sz.span, sz.heads * sz.seq), F32),
            pltpu.VMEM((sz.questions * sz.pad, sz.prefix * d), BF16),
            pltpu.VMEM((sz.questions * sz.pad, sz.prefix * d), BF16),
        ],
        compiler_params=params(),
        cost_estimate=COST,
        name="forward",
    )(tokens, wq, wk, wv, wo, gain1, gain2, table, mkeys, mvalues, ids, lengths, buckets)


def ffn_kernel(core, normed2, cot, wi, wo, act, d_inner, keep, send):
    block = 256
    n = normed2.shape[0]
    for r in range(0, n, block):
        rows = slice(r, r + block)
        v = nn(normed2[rows, :], wi[...])
        d_act = nt(cot[rows, :], wo[...])
        sq = v * v
        t = jnp.tanh(v * (GELU_C + (GELU_C * GELU_A) * sq))
        half = 0.5 + 0.5 * t
        act[rows, :] = (v * half).astype(BF16)
        slope = half + (0.5 * v) * (1.0 - t * t) * (GELU_C + (3.0 * GELU_C * GELU_A) * sq)
        d_inner[rows, :] = (d_act * slope).astype(BF16)

    @pl.when(core[0] == 0)
    def _():
        send[0] = tn(normed2[...], d_inner[...])
        keep[0] = tn(act[...], cot[...])

    @pl.when(core[0] != 0)
    def _():
        send[0] = tn(act[...], cot[...])
        keep[0] = tn(normed2[...], d_inner[...])


def ffn(core, normed2, cot, wi, wo, first, count):
    n, d = normed2.shape
    full = pl.BlockSpec((n, d), lambda j, c: (0, 0))
    cols = pl.BlockSpec((n, d), lambda j, c: (0, j))
    part = pl.BlockSpec((1, d, d), lambda j, c: (j, 0, 0))
    return pl.pallas_call(
        ffn_kernel,
        grid_spec=pltpu.PrefetchScalarGridSpec(
            num_scalar_prefetch=1,
            grid=(count,),
            in_specs=[
                full,
                full,
                pl.BlockSpec((d, d), lambda j, c: (0, first + j)),
                pl.BlockSpec((d, d), lambda j, c: (first + j, 0)),
            ],
            out_specs=[cols, cols, part, part],
        ),
        out_shape=[
            shape((n, count * d), BF16),
            shape((n, count * d), BF16),
            shape((count, d, d), F32),
            shape((count, d, d), F32),
        ],
        compiler_params=params(),
        cost_estimate=COST,
        name="ffn",
    )(core, normed2, cot, wi, wo)


def mid_kernel(
    steps, per, d_in0, d_in1, wi, hidden, cot, gain2, attended, wo,
    d_hidden, d_attended, grad_out, grad_gain, total,
):
    j = pl.program_id(0)
    block = 256
    n = hidden.shape[0]

    @pl.when(j == 0)
    def _():
        total[...] = nt(d_in0[...], wi[...])

    @pl.when(jnp.logical_and(j > 0, j < per))
    def _():
        total[...] += nt(d_in0[...], wi[...])

    @pl.when(j >= per)
    def _():
        total[...] += nt(d_in1[...], wi[...])

    @pl.when(j == steps - 1)
    def _():
        acc = jnp.zeros((1, hidden.shape[1]), F32)
        for r in range(0, n, block):
            rows = slice(r, r + block)
            h = hidden[rows, :]
            scale = lax.rsqrt(jnp.mean(h * h, axis=-1, keepdims=True) + EPS)
            base = h * scale
            d_normed = total[rows, :]
            scaled = d_normed * gain2[...].reshape(1, -1)
            acc = acc + jnp.sum(d_normed * base, axis=0, keepdims=True)
            back = scale * (scaled - base * jnp.mean(scaled * base, axis=-1, keepdims=True))
            d_h = cot[rows, :].astype(F32) + back
            d_hidden[rows, :] = d_h
            total[rows, :] = d_h
            d_attended[rows, :] = nt(d_h.astype(BF16), wo[...]).astype(BF16)
        grad_gain[...] = acc
        grad_out[...] = tn(attended[...], total[...].astype(BF16))


def mid(d_in0, d_in1, wi, hidden, cot, gain2, attended, wo):
    n, d = hidden.shape
    per = d_in0.shape[1] // d
    steps = 2 * per
    full = pl.BlockSpec((n, d), lambda j: (0, 0))
    square = pl.BlockSpec((d, d), lambda j: (0, 0))
    row = pl.BlockSpec((1, d), lambda j: (0, 0))
    gain = pl.BlockSpec((d,), lambda j: (0,))
    return pl.pallas_call(
        functools.partial(mid_kernel, steps, per),
        grid=(steps,),
        in_specs=[
            pl.BlockSpec((n, d), lambda j: (0, jnp.minimum(j, per - 1))),
            pl.BlockSpec((n, d), lambda j: (0, jnp.maximum(j - per, 0))),
            pl.BlockSpec((d, d), lambda j: (0, j)),
            full,
            full,
            gain,
            full,
            square,
        ],
        out_specs=[full, full, square, row],
        out_shape=[shape((n, d), F32), shape((n, d), BF16), shape((d, d), F32), shape((1, d), F32)],
        scratch_shapes=[pltpu.VMEM((n, d), F32)],
        compiler_params=params(),
        cost_estimate=COST,
        name="mid",
    )(d_in0, d_in1, wi, hidden, cot, gain2, attended, wo)


def back_kernel(
    sz,
    core, query, key, value, d_att, normed1, grad_out, mkeys, mvalues, ids, lengths, buckets, table,
    wq, wk, wv, gain1, grad_gain2,
    d_query, d_key, d_value, keep0, send0, keep1, send1,
    bias, memk, memv, d_memk, d_memv, d_bias, sums,
):
    d = sz.width
    pick = one_hot(ids, sz)
    fill_memory(pick, mkeys, memk)
    fill_memory(pick, mvalues, memv)
    fill_bias(bias, table, buckets, sz)
    d_bias[...] = jnp.zeros_like(d_bias)
    mask = head_mask(sz)

    def step(q, carry):
        length = lengths[q]
        rows = pl.ds(pl.multiple_of(q * sz.seq, sz.seq), sz.seq)
        mrows = pl.ds(pl.multiple_of(q * sz.pad, sz.pad), sz.pad)
        for c in range(sz.quads):
            col = c * sz.qw
            cols = slice(col, col + sz.qw)
            sq = spread(query[rows, cols], mask, sz)
            so = spread(d_att[rows, cols], mask, sz)
            keys = key_block(key, memk, q, col, sz)
            values = key_block(value, memv, q, col, sz)
            probs = probabilities(keys, sq, bias[:, cols], length, sz)
            d_probs = nt(values, so)
            d_val = nn(probs.astype(BF16), so)
            inner = jnp.sum(probs * d_probs, axis=0, keepdims=True)
            d_scores = (probs * (d_probs - inner)).astype(BF16)
            d_bias[:, cols] += d_scores[0 : sz.seq, :].astype(F32)
            d_query[rows, cols] = gather_diag(tn(d_scores, keys), sz).astype(BF16)
            d_ky = nn(d_scores, sq)
            d_key[rows, cols] = d_ky[0 : sz.seq, :].astype(BF16)
            d_value[rows, cols] = d_val[0 : sz.seq, :].astype(BF16)
            for p in range(sz.prefix):
                part = slice(sz.seq + p * sz.pad, sz.seq + (p + 1) * sz.pad)
                to = slice(p * d + col, p * d + col + sz.qw)
                d_memk[mrows, to] = d_ky[part, :]
                d_memv[mrows, to] = d_val[part, :]
        return carry

    lax.fori_loop(0, sz.questions, step, 0)

    def table_grad(full):
        high = full[...].astype(BF16)
        rest = (full[...] - high.astype(F32)).astype(BF16)
        return tn(pick, high) + tn(pick, rest)

    def emit(out, left, right, mem):
        out[0:d, :] = tn(left[...], right[...])
        grads = table_grad(mem)
        for p in range(sz.prefix):
            out[d + p * sz.entries : d + (p + 1) * sz.entries, :] = grads[:, p * d : (p + 1) * d]

    bt = bucket_lanes(buckets, sz)
    for pair in range(sz.heads // 2):
        cols = slice(pair * 2 * sz.seq, (pair + 1) * 2 * sz.seq)
        part = d_bias[:, cols]
        for b in range(sz.buckets):
            sums[b : b + 1, cols] = jnp.sum(jnp.where(bt == float(b), part, 0.0), axis=0, keepdims=True)
    width = sz.heads * sz.seq
    flat = sz.heads * sz.buckets
    head_in = lax.broadcasted_iota(jnp.int32, (width, d), 0) // sz.seq
    head_out = lax.broadcasted_iota(jnp.int32, (width, d), 1) // sz.buckets
    by_head = jnp.dot(
        sums[...], jnp.where(head_in == head_out, 1.0, 0.0),
        precision=lax.Precision.HIGHEST, preferred_element_type=F32,
    )
    own = lax.broadcasted_iota(jnp.int32, (sz.buckets, d), 0)
    lane = lax.broadcasted_iota(jnp.int32, (sz.buckets, d), 1)
    here = jnp.logical_and(lane % sz.buckets == own, lane < flat)
    bias_row = jnp.sum(jnp.where(here, by_head, 0.0), axis=0, keepdims=True)

    def small_rows(out, q_ref, k_ref, v_ref):
        terms = wq[...].astype(F32) * q_ref[0:d, :] + wk[...].astype(F32) * k_ref[0:d, :]
        terms = terms + wv[...].astype(F32) * v_ref[0:d, :]
        high = terms.astype(BF16)
        rest = (terms - high.astype(F32)).astype(BF16)
        ones = jnp.ones((8, d), BF16)
        total = (nt(ones, high) + nt(ones, rest))[0:1, :]
        out[d : d + SMALL, :] = jnp.zeros((SMALL, d), F32)
        out[d : d + 1, :] = total / gain1[...].reshape(1, -1)
        out[d + 1 : d + 2, :] = grad_gain2[...]
        out[d + 2 : d + 3, :] = bias_row

    @pl.when(core[0] == 0)
    def _():
        emit(send0, normed1, d_key, d_memv)
        emit(keep0, normed1, d_query, d_memk)
        send1[0:d, :] = grad_out[...]
        send1[d:, :] = jnp.zeros((SMALL, d), F32)
        keep1[0:d, :] = tn(normed1[...], d_value[...])
        small_rows(keep1, keep0, send0, keep1)

    @pl.when(core[0] != 0)
    def _():
        emit(send0, normed1, d_query, d_memk)
        emit(keep0, normed1, d_key, d_memv)
        send1[0:d, :] = tn(normed1[...], d_value[...])
        small_rows(send1, send0, keep0, send1)
        keep1[0:d, :] = grad_out[...]
        keep1[d:, :] = jnp.zeros((SMALL, d), F32)


def back(sz, core, query, key, value, d_att, normed1, grad_out, mkeys, mvalues, ids, lengths, buckets, table,
         wq, wk, wv, gain1, grad_gain2):
    n, d = sz.rows, sz.width
    low = shape((n, d), BF16)
    extra = sz.prefix * sz.entries
    mem = (sz.questions * sz.pad, sz.prefix * d)
    return pl.pallas_call(
        functools.partial(back_kernel, sz),
        in_specs=[SMEM] + [VMEM] * 9 + [SMEM] + [VMEM] * 7,
        out_specs=[VMEM] * 7,
        out_shape=[
            low,
            low,
            low,
            shape((d + extra, d), F32),
            shape((d + extra, d), F32),
            shape((d + SMALL, d), F32),
            shape((d + SMALL, d), F32),
        ],
        scratch_shapes=[
            pltpu.VMEM((sz.span, sz.heads * sz.seq), F32),
            pltpu.VMEM(mem, BF16),
            pltpu.VMEM(mem, BF16),
            pltpu.VMEM(mem, F32),
            pltpu.VMEM(mem, F32),
            pltpu.VMEM((sz.seq, sz.heads * sz.seq), F32),
            pltpu.VMEM((sz.buckets, sz.heads * sz.seq), F32),
        ],
        compiler_params=params(),
        cost_estimate=COST,
        name="back",
    )(core, query, key, value, d_att, normed1, grad_out, mkeys, mvalues, ids, lengths, buckets, table,
      wq, wk, wv, gain1, grad_gain2)


def last_kernel(tokens, d_hidden, gain1, d_query, d_key, d_value, wq, wk, wv, grad_tokens):
    block = 256
    for r in range(0, tokens.shape[0], block):
        rows = slice(r, r + block)
        d_normed = nt(d_query[rows, :], wq[...])
        d_normed = d_normed + nt(d_key[rows, :], wk[...])
        d_normed = d_normed + nt(d_value[rows, :], wv[...])
        x = tokens[rows, :].astype(F32)
        scale = lax.rsqrt(jnp.mean(x * x, axis=-1, keepdims=True) + EPS)
        base = x * scale
        scaled = d_normed * gain1[...].reshape(1, -1)
        back_in = scale * (scaled - base * jnp.mean(scaled * base, axis=-1, keepdims=True))
        grad_tokens[rows, :] = (d_hidden[rows, :] + back_in).astype(BF16)


def last(tokens, d_hidden, gain1, d_query, d_key, d_value, wq, wk, wv):
    n, d = tokens.shape
    return pl.pallas_call(
        last_kernel,
        in_specs=[VMEM] * 9,
        out_specs=VMEM,
        out_shape=shape((n, d), BF16),
        compiler_params=params(),
        cost_estimate=COST,
        name="last",
    )(tokens, d_hidden, gain1, d_query, d_key, d_value, wq, wk, wv)


def output_kernel(steps, per, hidden, act0, act1, wo, out, total):
    j = pl.program_id(0)

    @pl.when(j == 0)
    def _():
        total[...] = hidden[...] + nn(act0[...], wo[...])

    @pl.when(jnp.logical_and(j > 0, j < per))
    def _():
        total[...] += nn(act0[...], wo[...])

    @pl.when(jnp.logical_and(j >= per, j < steps - 1))
    def _():
        total[...] += nn(act1[...], wo[...])

    @pl.when(j == steps - 1)
    def _():
        out[...] = (total[...] + nn(act1[...], wo[...])).astype(BF16)


def output(hidden, act0, act1, wo):
    n, d = hidden.shape
    per = act0.shape[1] // d
    steps = 2 * per
    full = pl.BlockSpec((n, d), lambda j: (0, 0))
    return pl.pallas_call(
        functools.partial(output_kernel, steps, per),
        grid=(steps,),
        in_specs=[
            full,
            pl.BlockSpec((n, d), lambda j: (0, jnp.minimum(j, per - 1))),
            pl.BlockSpec((n, d), lambda j: (0, jnp.maximum(j - per, 0))),
            pl.BlockSpec((d, d), lambda j: (j, 0)),
        ],
        out_specs=full,
        out_shape=shape((n, d), BF16),
        scratch_shapes=[pltpu.VMEM((n, d), F32)],
        compiler_params=params(),
        cost_estimate=COST,
        name="output",
    )(hidden, act0, act1, wo)


CORE = ("dp", 1)
LINK_Y = ("dp", 2)
LINK_X = ("grp", 1)


def swap(value, link, sizes):
    axis, stride = link
    return lax.ppermute(value, axis, [(i, i ^ stride) for i in range(sizes[axis])])


def bit_of(link):
    axis, stride = link
    return (lax.axis_index(axis) // stride) % 2


def add_split_kernel(bits, *refs):
    count = len(refs) // 6
    for i in range(count):
        k0, r0, k1, r1 = refs[4 * i : 4 * i + 4]
        keep, send = refs[4 * count + 2 * i : 4 * count + 2 * i + 2]
        send[...] = k1[...].reshape(send.shape) + r1[...].reshape(send.shape)
        keep[...] = k0[...].reshape(keep.shape) + r0[...].reshape(keep.shape)


def add_split(bits, parts):
    steps = 2
    in_specs, out_specs, outs, operands = [], [], [], []
    for i, (kept, got, lead) in enumerate(parts):
        rows, d = kept.shape[-2:]
        rb = rows // 2 // steps
        for mine in (True, False):
            def index(j, b, i=i, mine=mine, lead=lead):
                half = b[i] if mine else 1 - b[i]
                place = (half * steps + j, 0)
                return place if lead is None else (lead,) + place

            spec = pl.BlockSpec((rb, d) if lead is None else (1, rb, d), index)
            in_specs += [spec, spec]
            operands += [kept, got]
            out_specs.append(pl.BlockSpec((rb, d), lambda j, b: (j, 0)))
            outs.append(shape((rows // 2, d), F32))
    total = sum(o.shape[0] * o.shape[1] for o in outs)
    result = pl.pallas_call(
        add_split_kernel,
        grid_spec=pltpu.PrefetchScalarGridSpec(
            num_scalar_prefetch=1, grid=(steps,), in_specs=in_specs, out_specs=out_specs
        ),
        out_shape=outs,
        compiler_params=params(),
        cost_estimate=COST,
        name="add_split",
    )(bits, *operands)
    return [(result[2 * i], result[2 * i + 1]) for i in range(len(parts))]


def add_pairs_kernel(a, b, c, d, out0, out1):
    out0[...] = a[...] + b[...]
    out1[...] = c[...] + d[...]


def add_pairs(a, b, c, d):
    return pl.pallas_call(
        add_pairs_kernel,
        in_specs=[VMEM] * 4,
        out_specs=[VMEM] * 2,
        out_shape=[shape(a.shape, F32), shape(c.shape, F32)],
        compiler_params=params(),
        cost_estimate=COST,
        name="add_pairs",
    )(a, b, c, d)


def join_kernel(bits, a, b, c, d, out0, out1):
    for first, own, got, out in ((0, a, b, out0), (1, c, d, out1)):
        n = own.shape[0]
        out[pl.ds(pl.multiple_of(bits[first] * n, 8), n), :] = own[...]
        out[pl.ds(pl.multiple_of((1 - bits[first]) * n, 8), n), :] = got[...]


def join(bits, a, b, c, d):
    return pl.pallas_call(
        join_kernel,
        in_specs=[SMEM] + [VMEM] * 4,
        out_specs=[VMEM] * 2,
        out_shape=[shape((2 * a.shape[0], a.shape[1]), F32), shape((2 * c.shape[0], c.shape[1]), F32)],
        compiler_params=params(),
        cost_estimate=COST,
        name="join",
    )(bits, a, b, c, d)


def rest_groups(size, low):
    return [[i for i in range(size) if i % low == r] for r in range(low)]


class Order:
    def __init__(self):
        self.done = None

    def after(self, value):
        if self.done is not None:
            value, _ = lax.optimization_barrier((value, self.done))
        return value

    def run(self, kernel, first, *rest):
        result = kernel(self.after(first), *rest)
        self.done = jax.tree.leaves(result)[0]
        return result


class Reduction:
    def __init__(self, order, sizes, turn_by, keep, send):
        self.order = order
        self.sizes = sizes
        self.turn_by = turn_by
        x_bit, y_bit = bit_of(LINK_X), bit_of(LINK_Y)
        self.xy = jnp.stack([x_bit, y_bit]).astype(jnp.int32)
        self.yx = jnp.stack([y_bit, x_bit]).astype(jnp.int32)
        self.place_bits = jnp.stack([bit_of(CORE), x_bit, y_bit]).astype(jnp.int32)
        self.kept = keep
        self.send = send

    def begin(self):
        moved = {}
        for array, _ in self.send:
            if id(array) not in moved:
                moved[id(array)] = swap(self.order.after(array), CORE, self.sizes)
        self.got = [(moved[id(array)], lead) for array, lead in self.send]

    def first(self):
        parts = [(k, g, lead) for (k, lead), (g, _) in zip(self.kept, self.got)]
        (self.k0, s0), (self.k1, s1) = self.order.run(add_split, self.xy, parts)
        self.r0, self.r1 = swap(s0, LINK_X, self.sizes), swap(s1, LINK_Y, self.sizes)

    def second(self):
        parts = [(self.k0, self.r0, None), (self.k1, self.r1, None)]
        (self.k0, s0), (self.k1, s1) = self.order.run(add_split, self.yx, parts)
        self.r0, self.r1 = swap(s0, LINK_Y, self.sizes), swap(s1, LINK_X, self.sizes)

    def third(self):
        pair = tuple(self.order.run(add_pairs, self.k0, self.r0, self.k1, self.r1))
        groups = rest_groups(self.sizes["dp"], 4)
        groups = groups[self.turn_by :] + groups[: self.turn_by]
        pair = lax.psum(pair, "dp", axis_index_groups=groups)
        if self.sizes["grp"] > 2:
            pair = lax.psum(pair, "grp", axis_index_groups=rest_groups(self.sizes["grp"], 2))
        self.pair = pair
        self.r0, self.r1 = swap(pair[0], LINK_Y, self.sizes), swap(pair[1], LINK_X, self.sizes)

    def fourth(self):
        g0, g1 = self.order.run(join, self.yx, self.pair[0], self.r0, self.pair[1], self.r1)
        h0, h1 = swap(g0, LINK_X, self.sizes), swap(g1, LINK_Y, self.sizes)
        self.own = (g0, h0, g1, h1)
        self.other = tuple(swap(v, CORE, self.sizes) for v in self.own)

    def finish(self, plan, outs, olds=()):
        olds = self.order.run(lambda bits: place(0, plan, bits, self.own, outs, olds), self.place_bits)
        return self.order.run(lambda bits: place(1, plan, bits, self.other, outs, olds), self.place_bits)


def place_kernel(other_core, plan, n_out, n_alias, bits, *refs):
    parts = refs[:4]
    outs = refs[4 + n_alias : 4 + n_alias + n_out]
    bufs = refs[4 + n_alias + n_out : 8 + n_alias + n_out]
    in_sems, out_sems = refs[-2:]
    loads = [pltpu.make_async_copy(parts[i], bufs[i], in_sems.at[i]) for i in range(4)]
    for load in loads:
        load.start()
    for load in loads:
        load.wait()
    for core in (0, 1):
        for x_bit in (0, 1):
            for y_bit in (0, 1):
                test = (bits[0] == core) & (bits[1] == x_bit) & (bits[2] == y_bit)

                @pl.when(test)
                def _(core=core, x_bit=x_bit, y_bit=y_bit):
                    copies = []
                    for index in range(4):
                        part, other_half = index // 2, index % 2
                        key = (part, core ^ other_core, (x_bit, y_bit)[part] ^ other_half)
                        for row, rows, out, where in plan[key]:
                            copies.append(
                                pltpu.make_async_copy(
                                    bufs[index].at[pl.ds(row, rows)],
                                    outs[out].at[where],
                                    out_sems.at[len(copies)],
                                )
                            )
                    for copy in copies:
                        copy.start()
                    for copy in copies:
                        copy.wait()


def place(other_core, plan, bits, arrays, outs, olds=()):
    n_copies = sum(len(v) for v in plan.values())
    return pl.pallas_call(
        functools.partial(place_kernel, other_core, plan, len(outs), len(olds)),
        in_specs=[SMEM] + [ANY] * (4 + len(olds)),
        out_specs=[ANY] * len(outs),
        out_shape=outs,
        input_output_aliases={5 + i: i for i in range(len(olds))},
        scratch_shapes=[pltpu.VMEM(a.shape, F32) for a in arrays]
        + [pltpu.SemaphoreType.DMA((4,)), pltpu.SemaphoreType.DMA((n_copies,))],
        compiler_params=params(),
        cost_estimate=COST,
        name="place",
    )(bits, *arrays, *olds)


def ffn_plan(first, d):
    plan = {}
    h = d // 2
    for part in (0, 1):
        at = (first + part) * d
        for half in (0, 1):
            plan[(part, 0, half)] = [(0, h, 0, (pl.ds(at + half * h, h), pl.ds(0, d)))]
            plan[(part, 1, half)] = [(0, h, 1, (pl.ds(half * h, h), pl.ds(at, d)))]
    return plan


def attn_plan(d, entries, prefix):
    plan = {}
    whole = pl.ds(0, d)
    for core, weight, mem in ((0, 0, 4), (1, 1, 5)):
        rows = d + prefix * entries
        h = rows // 2
        blocks = [(0, d, weight, 0)] + [(d + p * entries, entries, mem, p) for p in range(prefix)]
        for half in (0, 1):
            todo = []
            for start, count, out, p in blocks:
                low, high = max(start, half * h), min(start + count, (half + 1) * h)
                if low < high:
                    where = (pl.ds(low - start, high - low), pl.ds(p * d, d) if out >= 4 else whole)
                    todo.append((low - half * h, high - low, out, where))
            plan[(0, core, half)] = todo
    for core, blocks in ((0, [(0, d, 2), (d, SMALL, 6)]), (1, [(0, d, 3)])):
        h = (d + SMALL) // 2
        for half in (0, 1):
            todo = []
            for start, count, out in blocks:
                low, high = max(start, half * h), min(start + count, (half + 1) * h)
                if low < high:
                    todo.append((low - half * h, high - low, out, (pl.ds(low - start, high - low), whole)))
            plan[(1, core, half)] = todo
    return plan


def body(
    sizes,
    tokens,
    cotangent,
    w_query,
    w_key,
    w_value,
    w_attn_out,
    w_inner,
    w_outer,
    gain_attn,
    gain_ffn,
    bias_table,
    mem_keys,
    mem_values,
    mem_ids,
    lengths,
    buckets,
):
    questions, top = mem_ids.shape
    n, d = tokens.shape
    sz = Sizes(n, d, questions, bias_table.shape[1], bias_table.shape[0], mem_keys.shape[0], top, mem_keys.shape[1])
    core = bit_of(CORE).reshape(1).astype(jnp.int32)
    order = Order()
    half = w_inner.shape[1] // d // 2
    ffn_outs = [shape(w_outer.shape, F32), shape(w_inner.shape, F32)]
    square = shape((d, d), F32)
    mem = shape(mem_keys.shape, F32)

    normed1, query, key, value, attended, hidden, normed2 = order.run(
        functools.partial(forward, sz), tokens, w_query, w_key, w_value, w_attn_out, gain_attn, gain_ffn, bias_table,
        mem_keys, mem_values, mem_ids, lengths, buckets,
    )
    act0, d_in0, keep_a, send_a = order.run(ffn, core, normed2, cotangent, w_inner, w_outer, 0, half)
    red_a = Reduction(order, sizes, 0, [(keep_a, 0), (keep_a, 1)], [(send_a, 0), (send_a, 1)])
    red_a.begin()
    act1, d_in1, keep_b, send_b = order.run(ffn, core, normed2, cotangent, w_inner, w_outer, half, half)
    red_b = Reduction(order, sizes, 1, [(keep_b, 0), (keep_b, 1)], [(send_b, 0), (send_b, 1)])
    red_b.begin()
    red_a.first()
    d_hidden, d_attended, grad_out, grad_gain2 = order.run(
        mid, d_in0, d_in1, w_inner, hidden, cotangent, gain_ffn, attended, w_attn_out
    )
    red_b.first()
    red_a.second()
    d_query, d_key, d_value, keep0, send0, keep1, send1 = order.run(
        functools.partial(back, sz),
        core, query, key, value, d_attended, normed1, grad_out, mem_keys, mem_values,
        mem_ids, lengths, buckets, bias_table, w_query, w_key, w_value, gain_attn, grad_gain2,
    )
    red_c = Reduction(order, sizes, 2, [(keep0, None), (keep1, None)], [(send0, None), (send1, None)])
    red_a.third()
    red_c.begin()
    red_b.second()
    red_c.first()
    grad_tokens = order.run(
        last, tokens, d_hidden, gain_attn, d_query, d_key, d_value, w_query, w_key, w_value
    )
    red_b.third()
    red_a.fourth()
    out = order.run(output, hidden, act0, act1, w_outer)
    red_c.second()
    red_c.third()
    red_b.fourth()
    grads = red_a.finish(ffn_plan(0, d), ffn_outs)
    grad_w_outer, grad_w_inner = red_b.finish(ffn_plan(half, d), ffn_outs, grads)
    red_c.fourth()
    gq, gk, gv, go, gmk, gmv, small = red_c.finish(
        attn_plan(d, sz.entries, sz.prefix),
        [square, square, square, square, mem, mem, shape((SMALL, d), F32)],
    )
    return (
        out,
        grad_tokens,
        gq,
        gk,
        gv,
        go,
        grad_w_inner,
        grad_w_outer,
        small[0],
        small[1],
        small[2, : sz.heads * sz.buckets].reshape(sz.heads, sz.buckets).T,
        gmk,
        gmv,
    )


def solution(mesh):
    split = P(("grp", "dp"), None)
    placed = (split, split) + (P(),) * 11 + (split, P(("grp", "dp")), P())
    return jax.shard_map(
        functools.partial(body, dict(mesh.shape)),
        mesh=mesh,
        in_specs=placed,
        out_specs=(split, split) + (P(),) * 11,
        check_vma=False,
    )
```

time: 1720 us -> 506 us (0.29)
  waiting for transfers between devices: 1200 us -> 216 us
  local copies, waits for them, and re-layouts: 248 us -> 10.6 us
  Pallas kernels: 0 us -> 227 us
  matrix products: 146 us -> 0 us
  blocking collectives: 86.5 us -> 0 us
  starting transfers between devices: 0.31 us -> 31.6 us
    unnamed x9 -> x3, waiting for transfers between devices: 672 us -> 0.05 us
    all_gather x6 -> x0, waiting for transfers between devices: 251 us -> none  [the longest x1 116 us: reduce_ffn(): lax.all_gather(totals[0], 'grp', axis=0, tiled=True)]
    pallas_call x0 -> x25, Pallas kernels: none -> 227 us  [the longest x1 38.8 us: back(): pl.pallas_call(functools.partial(back_kernel, sz), in_specs=[SMEM] + [VME...]
    psum x1 -> x3, waiting for transfers between devices: 274 us -> 76.8 us  [third(): pair = lax.psum(pair, 'dp', axis_index_groups=groups)]
    dot_general x30 -> x0, matrix products: 146 us -> none  [the longest x8 36.8 us: matmul(): return jnp.dot(left, right, preferred_element_type=F32)]
    ppermute x0 -> x40, waiting for transfers between devices: none -> 139 us  [swap(): lax.ppermute(value, axis, [(i, i ^ stride) for i in range(sizes[axis])])]
    reshape x27 -> x0, local copies, waits for them, and re-layouts: 102 us -> none  [the longest x2 12.4 us: body(): query_heads = query.reshape(question_count, seq_len, head_count, head_size)]
    all_gather x4 -> x0, blocking collectives: 42 us -> none  [the longest x1 19.6 us: reduce_attn(): lax.all_gather(totals[4], 'grp', axis=0, tiled=True)]
  transfers between devices with their start and end apart: 8 -> 43, of which waited for: 5 -> 16; matrix products, arithmetic and copies ran while one was open for 4% -> 0% of each run, Pallas kernels for 0% -> 33%
where the time goes in v1:
time: 506 us; the launch traced here: 502 us
  Pallas kernels  227 us (45%)
  waiting for transfers between devices  216 us (43%)
  starting transfers between devices  31.6 us (6%)
  between operations  14.5 us (3%)
  local copies, waits for them, and re-layouts  10.6 us (2%)
    ppermute x40, waiting for transfers between devices, swap(): lax.ppermute(value, axis, [(i, i ^ stride) for i in range(sizes[axis])])  139 us
    psum x3, waiting for transfers between devices, third(): pair = lax.psum(pair, 'dp', axis_index_groups=groups)  76.8 us
    pallas_call x1, Pallas kernels, back(): pl.pallas_call(functools.partial(back_kernel, sz), in_specs=[SMEM] + [VME...  38.8 us
    pallas_call x2, Pallas kernels, ffn(): pl.pallas_call(ffn_kernel, grid_spec=pltpu.PrefetchScalarGridSpec(num_sca...  34.7 us
    pallas_call x6, Pallas kernels, add_split(): pl.pallas_call(add_split_kernel, grid_spec=pltpu.PrefetchScalarGridSpec(n...  34 us
    pallas_call x6, Pallas kernels, place(): pl.pallas_call(functools.partial(place_kernel, other_core, plan, len(outs...  32.9 us
    ppermute x40, starting transfers between devices, swap(): lax.ppermute(value, axis, [(i, i ^ stride) for i in range(sizes[axis])])  31.2 us
    pallas_call x1, Pallas kernels, forward(): pl.pallas_call(functools.partial(forward_kernel, sz), in_specs=[VMEM] * 1...  30.4 us
  transfers between devices with their start and end apart: 43, of which 16 were waited for; matrix products, arithmetic and copies ran while one was open for 0% of the time, Pallas kernels for 33%

profile of v1, /device:TPU:0, one launch (start us, length us, event | category | flops | bytes accessed | tf_op | source)
XLA Modules:
  0.0 501.6 jit_solution(9284299199363797504)
XLA Ops:
  8.6 30.4 %forward.1 = (bf16[1024,768]{1,0:T(8,128)(2,1)}, bf16[1024,768]{1,0:T(8,128)(2,1)}, bf16[1024,768]{1,0:T(8,128)(2,1)}, bf16[1024,768]{1,0:T(8,128)(2,1)}, bf16[1...) custom-call(bf16[1024,768]{1,0:T(8,128)(2,1)} %tokens.2, bf16[768,768]{1,0:T(8,128)(2,1)} %wq.5, ...), custom_call_target="tpu_custom_call" | custom-call | flops 1 | bytes 1 | tf_op jit(solution)/shard_map/forward/pallas_call | solution.py:195
  39.0 17.2 %ffn.2 = (bf16[1024,1536]{1,0:T(8,128)(2,1)}, bf16[1024,1536]{1,0:T(8,128)(2,1)}, f32[2,768,768]{2,1,0:T(8,128)}, f32[2,768,768]{2,1,0:T(8,128)}) custom-call(s32[1]{0:T(128)} %bitcast.2.core, bf16[1024,768]{1,0:T(8,128)(2,1)} %get-tuple-element.127.normed2, bf16[1024,768]{1,0:T(8,128)(2,1)} %cot.5, bf16[768,3072]{1,0:T(8,128)(2,1)} %wi.5, bf16[3072,768]{1,0:T(8,128)(2,1)} %wo.9), custom_call_target="tpu_custom_call" | custom-call | flops 1 | bytes 1 | tf_op jit(solution)/shard_map/ffn/pallas_call | solution.py:241
  56.6 17.6 %ffn.3 = (bf16[1024,1536]{1,0:T(8,128)(2,1)}, bf16[1024,1536]{1,0:T(8,128)(2,1)}, f32[2,768,768]{2,1,0:T(8,128)}, f32[2,768,768]{2,1,0:T(8,128)}) custom-call(s32[1]{0:T(128)} %bitcast.2.core, bf16[1024,768]{1,0:T(8,128)(2,1)} %get-tuple-element.127.normed2, bf16[1024,768]{1,0:T(8,128)(2,1)} %cot.5, bf16[768,3072]{1,0:T(8,128)(2,1)} %wi.5, bf16[3072,768]{1,0:T(8,128)(2,1)} %wo.9), custom_call_target="tpu_custom_call" | custom-call | flops 1 | bytes 1 | tf_op jit(solution)/shard_map/ffn/pallas_call | solution.py:241
  74.9 6.5 %add_split.6 = (f32[384,768]{1,0:T(8,128)}, f32[384,768]{1,0:T(8,128)}, f32[384,768]{1,0:T(8,128)}, f32[384,768]{1,0:T(8,128)}) custom-call(s32[2]{0:T(128)} %pad_add_fusion.1.bits, f32[2,768,768]{2,1,0:T(8,128)} %get-tuple-element.133.refs_0_.refs_2_.refs_4_.refs_6_, f32[2,768,768]{2,1,0:T(8,128)} %collective-permute-done.refs_1_.refs_3_.refs_5_.refs_7_, ...), custom_call_target="tpu_custom_call" | custom-call | flops 1 | bytes 1 | tf_op jit(solution)/shard_map/add_split/pallas_call | solution.py:590
  81.4 3.0 collective-permute-start.2
  84.4 1.5 collective-permute-start.3
  86.5 17.3 %mid.1 = (f32[1024,768]{1,0:T(8,128)}, bf16[1024,768]{1,0:T(8,128)(2,1)}, f32[768,768]{1,0:T(8,128)}, f32[1,768]{1,0:T(1,128)}) custom-call(bf16[1024,1536]{1,0:T(8,128)(2,1)} %get-tuple-element.137.d_in0, bf16[1024,1536]{1,0:T(8,128)(2,1)} %get-tuple-element.138.d_in1, bf16[768,3072]{1,0:T(8,128)(2,1)} %wi.5, f32[1024,768]{1,0:T(8,128)} %get-tuple-element.188.hidden, ...), custom_call_target="tpu_custom_call" | custom-call | flops 1 | bytes 1 | tf_op jit(solution)/shard_map/mid/pallas_call | solution.py:314
  103.8 6.6 %add_split.7 = (f32[384,768]{1,0:T(8,128)}, f32[384,768]{1,0:T(8,128)}, f32[384,768]{1,0:T(8,128)}, f32[384,768]{1,0:T(8,128)}) custom-call(s32[2]{0:T(128)} %pad_add_fusion.1.bits, f32[2,768,768]{2,1,0:T(8,128)} %get-tuple-element.142.refs_0_.refs_2_.refs_4_.refs_6_, f32[2,768,768]{2,1,0:T(8,128)} %collective-permute-done.1.refs_1_.refs_3_.refs_5_.refs_7_, ...), custom_call_target="tpu_custom_call" | custom-call | flops 1 | bytes 1 | tf_op jit(solution)/shard_map/add_split/pallas_call | solution.py:590
  113.3 4.2 add_split.8
  117.5 1.6 collective-permute-start.4
  119.7 38.8 %back.1 = (bf16[1024,768]{1,0:T(8,128)(2,1)}, bf16[1024,768]{1,0:T(8,128)(2,1)}, bf16[1024,768]{1,0:T(8,128)(2,1)}, f32[1024,768]{1,0:T(8,128)}, f32[1024,768]{1...) custom-call(s32[1]{0:T(128)} %bitcast.2.core, bf16[1024,768]{1,0:T(8,128)(2,1)} %get-tuple-element.152.query, ...), custom_call_target="tpu_custom_call" | custom-call | flops 1 | bytes 1 | tf_op jit(solution)/shard_map/back/pallas_call | solution.py:448
  159.6 2.7 add_pairs.3
  164.7 26.2 %collective-permute-done.6.refs_1_.refs_3_ = f32[384,768]{1,0:T(8,128)} collective-permute-done((f32[384,768]{1,0:T(8,128)}, f32[384,768]{1,0:T(8,128)}, u32[]{:S(2)}, u32[]{:S(2)}) %collective-permute-start.6) | collective-permute-done | bytes 1179680 | tf_op jit(solution)/shard_map/ppermute | solution.py:555
  192.1 4.2 add_split.9
  196.8 1.6 copy-done
  198.5 8.0 %add_split.10 = (f32[512,768]{1,0:T(8,128)}, f32[512,768]{1,0:T(8,128)}, f32[416,768]{1,0:T(8,128)}, f32[416,768]{1,0:T(8,128)}) custom-call(s32[2]{0:T(128)} %pad_add_fusion.1.bits, f32[1024,768]{1,0:T(8,128)} %get-tuple-element.170.refs_0_.refs_2_, f32[1024,768]{1,0:T(8,128)} %copy-done, f32[1024,768]{1,0:T(8,128)} %get-tuple-element.170.refs_0_.refs_2_, ...), custom_call_target="tpu_custom_call" | custom-call | flops 1 | bytes 1 | tf_op jit(solution)/shard_map/add_split/pallas_call | solution.py:590
  207.3 1.5 collective-permute-start.15
  210.1 11.4 %all-reduce.7.cloned.1.call-done = (f32[192,768]{1,0:T(8,128)}, f32[192,768]{1,0:T(8,128)}) async-done(((f32[192,768]{1,0:T(8,128)}, f32[192,768]{1,0:T(8,128)}), (f32[192,768]{1,0:T(8,128)}, f32[192,768]{1,0:T(8,128)})) %all-reduce.7.cloned.1.call-update) | async-done | bytes 1179664 | tf_op jit(solution)/shard_map/psum | solution.py:691
  221.5 1.5 collective-permute-start.12
  223.0 1.5 collective-permute-start.13
  224.5 10.3 %last.1 = bf16[1024,768]{1,0:T(8,128)(2,1)} custom-call(bf16[1024,768]{1,0:T(8,128)(2,1)} %tokens.2, f32[1024,768]{1,0:T(8,128)} %get-tuple-element.140.d_hidden, f32[768]{0:T(1024)} %gain1.5, bf16[1024,768]{1,0:T(8,128)(2,1)} %get-tuple-element.158.d_query, bf16[1024,768]{1,0:T(8,128)(2,1)} %get-tuple-element.178.d_key, ...), custom_call_target="tpu_custom_call" | custom-call | flops 1 | bytes 1 | tf_op jit(solution)/shard_map/last/pallas_call | solution.py:494
  234.8 22.1 %collective-permute-done.11.d = f32[192,768]{1,0:T(8,128)} collective-permute-done((f32[192,768]{1,0:T(8,128)}, f32[192,768]{1,0:T(8,128)}, u32[]{:S(2)}, u32[]{:S(2)}) %collective-permute-start.11) | collective-permute-done | bytes 589856 | tf_op jit(solution)/shard_map/ppermute | solution.py:555
  256.8 2.7 add_pairs.4
  259.5 7.5 %collective-permute-done.13.d = f32[192,768]{1,0:T(8,128)} collective-permute-done((f32[192,768]{1,0:T(8,128)}, f32[192,768]{1,0:T(8,128)}, u32[]{:S(2)}, u32[]{:S(2)}) %collective-permute-start.13) | collective-permute-done | bytes 589856 | tf_op jit(solution)/shard_map/ppermute | solution.py:555
  267.1 3.1 join.3
  271.1 10.4 %output.1 = bf16[1024,768]{1,0:T(8,128)(2,1)} custom-call(f32[1024,768]{1,0:T(8,128)} %get-tuple-element.188.hidden, bf16[1024,1536]{1,0:T(8,128)(2,1)} %get-tuple-element.129.act0, bf16[1024,1536]{1,0:T(8,128)(2,1)} %get-tuple-element.131.act1, bf16[3072,768]{1,0:T(8,128)(2,1)} %wo.9), custom_call_target="tpu_custom_call" | custom-call | flops 1 | bytes 1 | tf_op jit(solution)/shard_map/output/pallas_call | solution.py:530
  283.1 4.6 add_split.11
  287.7 1.7 collective-permute-start.16
  291.3 8.1 %collective-permute-done.20.refs_1_ = f32[384,768]{1,0:T(8,128)} collective-permute-done((f32[384,768]{1,0:T(8,128)}, f32[384,768]{1,0:T(8,128)}, u32[]{:S(2)}, u32[]{:S(2)}) %collective-permute-start.20) | collective-permute-done | bytes 1179680 | tf_op jit(solution)/shard_map/ppermute | solution.py:555
  299.4 29.0 %all-reduce.9.cloned.1.call-done = (f32[192,768]{1,0:T(8,128)}, f32[192,768]{1,0:T(8,128)}) async-done(((f32[192,768]{1,0:T(8,128)}, f32[192,768]{1,0:T(8,128)}), (f32[192,768]{1,0:T(8,128)}, f32[192,768]{1,0:T(8,128)})) %all-reduce.9.cloned.1.call-update) | async-done | bytes 1179664 | tf_op jit(solution)/shard_map/psum | solution.py:691
  328.4 1.5 collective-permute-start.18
  329.9 1.5 collective-permute-start.19
  331.4 2.9 add_pairs.5
  334.3 9.7 %collective-permute-done.18.b = f32[192,768]{1,0:T(8,128)} collective-permute-done((f32[192,768]{1,0:T(8,128)}, f32[192,768]{1,0:T(8,128)}, u32[]{:S(2)}, u32[]{:S(2)}) %collective-permute-start.18) | collective-permute-done | bytes 589856 | tf_op jit(solution)/shard_map/ppermute | solution.py:555
  345.2 3.1 join.4
  348.4 1.5 collective-permute-start.26
  351.1 24.6 %collective-permute-done.26.refs_1_ = f32[384,768]{1,0:T(8,128)S(1)} collective-permute-done((f32[384,768]{1,0:T(8,128)}, f32[384,768]{1,0:T(8,128)S(1)}, u32[]{:S(2)}, u32[]{:S(2)}) %collective-permute-start.26) | collective-permute-done | bytes 1179680 | tf_op jit(solution)/shard_map/ppermute | solution.py:555
  377.1 36.4 %all-reduce.11.cloned.1.call-done = (f32[256,768]{1,0:T(8,128)}, f32[208,768]{1,0:T(8,128)}) async-done(((f32[256,768]{1,0:T(8,128)}, f32[208,768]{1,0:T(8,128)}), (f32[256,768]{1,0:T(8,128)}, f32[208,768]{1,0:T(8,128)})) %all-reduce.11.cloned.1.call-update) | async-done | bytes 1425424 | tf_op jit(solution)/shard_map/psum | solution.py:691
  413.4 1.5 collective-permute-start.32
  414.9 1.5 collective-permute-start.33
  417.0 5.3 %place.6 = (f32[3072,768]{1,0:T(8,128)}, f32[768,3072]{1,0:T(8,128)}) custom-call(s32[3]{0:T(128)} %pad_add_fusion.2.bits, f32[384,768]{1,0:T(8,128)} %get-tuple-element.187.refs_0_, f32[384,768]{1,0:T(8,128)} %collective-permute-done.20.refs_1_, f32[384,768]{1,0:T(8,128)} %get-tuple-element.202.refs_2_, f32[384,768]{1,0:T(8,128)} %collective-permute-done.21.refs_3_), custom_call_target="tpu_custom_call" | custom-call | flops 1 | bytes 1 | tf_op jit(solution)/shard_map/place/pallas_call | solution.py:745
  422.3 5.3 %place.7 = (f32[3072,768]{1,0:T(8,128)}, f32[768,3072]{1,0:T(8,128)}) custom-call(s32[3]{0:T(128)} %pad_add_fusion.2.bits, f32[384,768]{1,0:T(8,128)} %copy-done.7, f32[384,768]{1,0:T(8,128)} %collective-permute-done.23.refs_1_, f32[384,768]{1,0:T(8,128)} %copy-done.8, ...), custom_call_target="tpu_custom_call", output_to_operand_aliasing={{0}: (5, {}), {1}: (6, {})} | custom-call | flops 1 | bytes 1 | tf_op jit(solution)/shard_map/place/pallas_call | solution.py:745
  427.6 5.3 %place.8 = (f32[3072,768]{1,0:T(8,128)}, f32[768,3072]{1,0:T(8,128)}) custom-call(s32[3]{0:T(128)} %pad_add_fusion.2.bits, f32[384,768]{1,0:T(8,128)} %get-tuple-element.200.refs_0_, f32[384,768]{1,0:T(8,128)} %copy-done.9, f32[384,768]{1,0:T(8,128)} %get-tuple-element.208.refs_2_, ...), custom_call_target="tpu_custom_call", output_to_operand_aliasing={{0}: (5, {}), {1}: (6, {})} | custom-call | flops 1 | bytes 1 | tf_op jit(solution)/shard_map/place/pallas_call | solution.py:745
  432.9 5.3 %place.9 = (f32[3072,768]{1,0:T(8,128)}, f32[768,3072]{1,0:T(8,128)}) custom-call(s32[3]{0:T(128)} %pad_add_fusion.2.bits, f32[384,768]{1,0:T(8,128)} %collective-permute-done.28.refs_0_, f32[384,768]{1,0:T(8,128)} %collective-permute-done.29.refs_1_, f32[384,768]{1,0:T(8,128)} %collective-permute-done.30.refs_2_, ...), custom_call_target="tpu_custom_call", output_to_operand_aliasing={{0}: (5, {}), {1}: (6, {})} | custom-call | flops 1 | bytes 1 | tf_op jit(solution)/shard_map/place/pallas_call | solution.py:745
  438.2 3.5 join.5
  442.8 34.5 %collective-permute-done.34.refs_1_ = f32[512,768]{1,0:T(8,128)} collective-permute-done((f32[512,768]{1,0:T(8,128)}, f32[512,768]{1,0:T(8,128)}, u32[]{:S(2)}, u32[]{:S(2)}) %collective-permute-start.34) | collective-permute-done | bytes 1572896 | tf_op jit(solution)/shard_map/ppermute | solution.py:555
  477.9 5.9 %place.10 = (f32[768,768]{1,0:T(8,128)}, f32[768,768]{1,0:T(8,128)}, f32[768,768]{1,0:T(8,128)}, f32[768,768]{1,0:T(8,128)}, f32[128,1536]{1,0:T(8,128)}, /*index=5*/f32[128,1536]{1,0:T(8,128)}, f32[64,768]{1,0:T(8,128)}) custom-call(s32[3]{0:T(128)} %pad_add_fusion.2.bits, f32[512,768]{1,0:T(8,128)} %get-tuple-element.216.refs_0_, ...), custom_call_target="tpu_custom_call" | custom-call | flops 1 | bytes 1 | tf_op jit(solution)/shard_map/place/pallas_call | solution.py:745
  485.9 5.9 %place.11 = (f32[768,768]{1,0:T(8,128)}, f32[768,768]{1,0:T(8,128)}, f32[768,768]{1,0:T(8,128)}, f32[768,768]{1,0:T(8,128)}, f32[128,1536]{1,0:T(8,128)}, /*index=5*/f32[128,1536]{1,0:T(8,128)}, f32[64,768]{1,0:T(8,128)}) custom-call(s32[3]{0:T(128)} %pad_add_fusion.2.bits, ...), custom_call_target="tpu_custom_call", output_to_operand_aliasing={{0}: (5, {}), {1}: (6, {}), {2}: (7, {}), {3}: (8, {}), {4}... | custom-call | flops 1 | bytes 1 | tf_op jit(solution)/shard_map/place/pallas_call | solution.py:745
  (101 shorter events, 29.3 us)
Async XLA Ops:
  7.2 214.3 %all-reduce.7.cloned.1.call-start = ((), (), s32[]{:S(2)}) async-start(), calls=%async_computation | async-start | bytes 2359296 | tf_op jit(solution)/shard_map/psum | solution.py:691
  56.2 18.7 %collective-permute-start = (f32[2,768,768]{2,1,0:T(8,128)}, f32[2,768,768]{2,1,0:T(8,128)}, u32[]{:S(2)}, u32[]{:S(2)}) collective-permute-start(f32[2,768,768]{2,1,0:T(8,128)} %get-tuple-element.135), channel_id=1, source_target_pairs={{0,1},{1,0},{2,3},{3,2},{4,5},{5,4},{6,7},{7,6},{8,9},{9,8},{10,11... | collective-permute-start | bytes 14155784 | tf_op jit(solution)/shard_map/ppermute | solution.py:555
  74.2 29.6 %collective-permute-start.1 = (f32[2,768,768]{2,1,0:T(8,128)}, f32[2,768,768]{2,1,0:T(8,128)}, u32[]{:S(2)}, u32[]{:S(2)}) collective-permute-start(f32[2,768,768]{2,1,0:T(8,128)} %get-tuple-element.144), channel_id=1, source_target_pairs={{0,1},{1,0},{2,3},{3,2},{4,5},{5,4},{6,7},{7,6},{8,9},{9,8},{10,11... | collective-permute-start | bytes 14155784 | tf_op jit(solution)/shard_map/ppermute | solution.py:555
  81.4 29.4 %collective-permute-start.2 = (f32[384,768]{1,0:T(8,128)}, f32[384,768]{1,0:T(8,128)S(1)}, u32[]{:S(2)}, u32[]{:S(2)}) collective-permute-start(f32[384,768]{1,0:T(8,128)} %get-tuple-element.147), channel_id=1, source_target_pairs={{0,16},{16,0},{1,17},{17,1},{2,18},{18,2},{3,19},{19,3},{4,20},{20... | collective-permute-start | bytes 3538952 | tf_op jit(solution)/shard_map/ppermute | solution.py:555
  84.4 27.9 %collective-permute-start.3 = (f32[384,768]{1,0:T(8,128)}, f32[384,768]{1,0:T(8,128)S(1)}, u32[]{:S(2)}, u32[]{:S(2)}) collective-permute-start(f32[384,768]{1,0:T(8,128)} %get-tuple-element.149), channel_id=1, source_target_pairs={{0,2},{1,3},{2,0},{3,1},{4,6},{5,7},{6,4},{7,5},{8,10},{9,11},{10,... | collective-permute-start | bytes 3538952 | tf_op jit(solution)/shard_map/ppermute | solution.py:555
  117.5 41.1 %collective-permute-start.4 = (f32[192,768]{1,0:T(8,128)}, f32[192,768]{1,0:T(8,128)S(1)}, u32[]{:S(2)}, u32[]{:S(2)}) collective-permute-start(f32[192,768]{1,0:T(8,128)} %get-tuple-element.160), channel_id=1, source_target_pairs={{0,2},{1,3},{2,0},{3,1},{4,6},{5,7},{6,4},{7,5},{8,10},{9,11},{10,... | collective-permute-start | bytes 1769480 | tf_op jit(solution)/shard_map/ppermute | solution.py:555
  119.1 39.5 %collective-permute-start.5 = (f32[192,768]{1,0:T(8,128)}, f32[192,768]{1,0:T(8,128)S(1)}, u32[]{:S(2)}, u32[]{:S(2)}) collective-permute-start(f32[192,768]{1,0:T(8,128)} %get-tuple-element.162), channel_id=1, source_target_pairs={{0,16},{16,0},{1,17},{17,1},{2,18},{18,2},{3,19},{19,3},{4,20},{20... | collective-permute-start | bytes 1769480 | tf_op jit(solution)/shard_map/ppermute | solution.py:555
  162.3 34.6 %collective-permute-start.8 = (f32[1024,768]{1,0:T(8,128)}, f32[1024,768]{1,0:T(8,128)S(1)}, u32[]{:S(2)}, u32[]{:S(2)}) collective-permute-start(f32[1024,768]{1,0:T(8,128)} %get-tuple-element.172), channel_id=1, source_target_pairs={{0,1},{1,0},{2,3},{3,2},{4,5},{5,4},{6,7},{7,6},{8,9},{9,8},{10,11... | collective-permute-start | bytes 9437192 | tf_op jit(solution)/shard_map/ppermute | solution.py:555
  162.3 34.6 %collective-permute-start.9 = (f32[832,768]{1,0:T(8,128)}, f32[832,768]{1,0:T(8,128)}, u32[]{:S(2)}, u32[]{:S(2)}) collective-permute-start(f32[832,768]{1,0:T(8,128)} %get-tuple-element.175), channel_id=1, source_target_pairs={{0,1},{1,0},{2,3},{3,2},{4,5},{5,4},{6,7},{7,6},{8,9},{9,8},{10,11... | collective-permute-start | bytes 7667720 | tf_op jit(solution)/shard_map/ppermute | solution.py:555
  162.8 28.2 %collective-permute-start.6 = (f32[384,768]{1,0:T(8,128)}, f32[384,768]{1,0:T(8,128)}, u32[]{:S(2)}, u32[]{:S(2)}) collective-permute-start(f32[384,768]{1,0:T(8,128)} %get-tuple-element.165), channel_id=1, source_target_pairs={{0,16},{16,0},{1,17},{17,1},{2,18},{18,2},{3,19},{19,3},{4,20},{20... | collective-permute-start | bytes 3538952 | tf_op jit(solution)/shard_map/ppermute | solution.py:555
  164.1 27.9 %collective-permute-start.7 = (f32[384,768]{1,0:T(8,128)}, f32[384,768]{1,0:T(8,128)}, u32[]{:S(2)}, u32[]{:S(2)}) collective-permute-start(f32[384,768]{1,0:T(8,128)} %get-tuple-element.167), channel_id=1, source_target_pairs={{0,2},{1,3},{2,0},{3,1},{4,6},{5,7},{6,4},{7,5},{8,10},{9,11},{10,... | collective-permute-start | bytes 3538952 | tf_op jit(solution)/shard_map/ppermute | solution.py:555
  164.7 163.8 %all-reduce.9.cloned.1.call-start = ((), (), s32[]{:S(2)}) async-start(), calls=%async_computation.1 | async-start | bytes 2359296 | tf_op jit(solution)/shard_map/psum | solution.py:691
  196.2 26.8 %collective-permute-start.10 = (f32[192,768]{1,0:T(8,128)}, f32[192,768]{1,0:T(8,128)}, u32[]{:S(2)}, u32[]{:S(2)}) collective-permute-start(f32[192,768]{1,0:T(8,128)} %get-tuple-element.181), channel_id=1, source_target_pairs={{0,2},{1,3},{2,0},{3,1},{4,6},{5,7},{6,4},{7,5},{8,10},{9,11},{10,... | collective-permute-start | bytes 1769480 | tf_op jit(solution)/shard_map/ppermute | solution.py:555
  196.8 1.6 copy-start
  206.5 75.1 %collective-permute-start.14 = (f32[512,768]{1,0:T(8,128)}, f32[512,768]{1,0:T(8,128)S(1)}, u32[]{:S(2)}, u32[]{:S(2)}) collective-permute-start(f32[512,768]{1,0:T(8,128)} %get-tuple-element.190), channel_id=1, source_target_pairs={{0,16},{16,0},{1,17},{17,1},{2,18},{18,2},{3,19},{19,3},{4,20},{20... | collective-permute-start | bytes 4718600 | tf_op jit(solution)/shard_map/ppermute | solution.py:555
  207.3 74.3 %collective-permute-start.15 = (f32[416,768]{1,0:T(8,128)}, f32[416,768]{1,0:T(8,128)S(1)}, u32[]{:S(2)}, u32[]{:S(2)}) collective-permute-start(f32[416,768]{1,0:T(8,128)} %get-tuple-element.192), channel_id=1, source_target_pairs={{0,2},{1,3},{2,0},{3,1},{4,6},{5,7},{6,4},{7,5},{8,10},{9,11},{10,... | collective-permute-start | bytes 3833864 | tf_op jit(solution)/shard_map/ppermute | solution.py:555
  208.8 48.0 %collective-permute-start.11 = (f32[192,768]{1,0:T(8,128)}, f32[192,768]{1,0:T(8,128)}, u32[]{:S(2)}, u32[]{:S(2)}) collective-permute-start(f32[192,768]{1,0:T(8,128)} %get-tuple-element.183), channel_id=1, source_target_pairs={{0,16},{16,0},{1,17},{17,1},{2,18},{18,2},{3,19},{19,3},{4,20},{20... | collective-permute-start | bytes 1769480 | tf_op jit(solution)/shard_map/ppermute | solution.py:555
  221.5 38.0 %collective-permute-start.12 = (f32[192,768]{1,0:T(8,128)}, f32[192,768]{1,0:T(8,128)S(1)}, u32[]{:S(2)}, u32[]{:S(2)}) collective-permute-start(f32[192,768]{1,0:T(8,128)} %get-tuple-element.237.a), channel_id=1, source_target_pairs={{0,2},{1,3},{2,0},{3,1},{4,6},{5,7},{6,4},{7,5},{8,10},{9,11},{10,... | collective-permute-start | bytes 1769480 | tf_op jit(solution)/shard_map/ppermute | solution.py:555
  223.0 44.1 %collective-permute-start.13 = (f32[192,768]{1,0:T(8,128)}, f32[192,768]{1,0:T(8,128)}, u32[]{:S(2)}, u32[]{:S(2)}) collective-permute-start(f32[192,768]{1,0:T(8,128)} %get-tuple-element.238.c), channel_id=1, source_target_pairs={{0,16},{16,0},{1,17},{17,1},{2,18},{18,2},{3,19},{19,3},{4,20},{20... | collective-permute-start | bytes 1769480 | tf_op jit(solution)/shard_map/ppermute | solution.py:555
  259.5 7.5 %copy-start.11 = (f32[192,768]{1,0:T(8,128)}, f32[192,768]{1,0:T(8,128)S(1)}, u32[]{:S(2)}) copy-start(f32[192,768]{1,0:T(8,128)S(1)} %collective-permute-done.12.b) | copy-start | bytes 1769476
  270.2 29.2 %collective-permute-start.20 = (f32[384,768]{1,0:T(8,128)}, f32[384,768]{1,0:T(8,128)}, u32[]{:S(2)}, u32[]{:S(2)}) collective-permute-start(f32[384,768]{1,0:T(8,128)} %get-tuple-element.187.refs_0_), channel_id=1, source_target_pairs={{0,16},{16,0},{1,17},{17,1},{2,18},{18,2},{3,19},{19,3},{4,20},{20... | collective-permute-start | bytes 3538952 | tf_op jit(solution)/shard_map/ppermute | solution.py:555
  270.8 142.6 %all-reduce.11.cloned.1.call-start = ((), (), s32[]{:S(2)}) async-start(), calls=%async_computation.2 | async-start | bytes 2850816 | tf_op jit(solution)/shard_map/psum | solution.py:691
  287.7 42.2 %collective-permute-start.16 = (f32[256,768]{1,0:T(8,128)}, f32[256,768]{1,0:T(8,128)S(1)}, u32[]{:S(2)}, u32[]{:S(2)}) collective-permute-start(f32[256,768]{1,0:T(8,128)} %get-tuple-element.194), channel_id=1, source_target_pairs={{0,2},{1,3},{2,0},{3,1},{4,6},{5,7},{6,4},{7,5},{8,10},{9,11},{10,... | collective-permute-start | bytes 2359304 | tf_op jit(solution)/shard_map/ppermute | solution.py:555
  289.4 39.1 %collective-permute-start.17 = (f32[208,768]{1,0:T(8,128)}, f32[208,768]{1,0:T(8,128)}, u32[]{:S(2)}, u32[]{:S(2)}) collective-permute-start(f32[208,768]{1,0:T(8,128)} %get-tuple-element.196), channel_id=1, source_target_pairs={{0,16},{16,0},{1,17},{17,1},{2,18},{18,2},{3,19},{19,3},{4,20},{20... | collective-permute-start | bytes 1916936 | tf_op jit(solution)/shard_map/ppermute | solution.py:555
  290.8 59.0 %collective-permute-start.21 = (f32[384,768]{1,0:T(8,128)}, f32[384,768]{1,0:T(8,128)}, u32[]{:S(2)}, u32[]{:S(2)}) collective-permute-start(f32[384,768]{1,0:T(8,128)} %get-tuple-element.202.refs_2_), channel_id=1, source_target_pairs={{0,2},{1,3},{2,0},{3,1},{4,6},{5,7},{6,4},{7,5},{8,10},{9,11},{10,... | collective-permute-start | bytes 3538952 | tf_op jit(solution)/shard_map/ppermute | solution.py:555
  291.3 59.1 %collective-permute-start.22 = (f32[384,768]{1,0:T(8,128)}, f32[384,768]{1,0:T(8,128)S(1)}, u32[]{:S(2)}, u32[]{:S(2)}) collective-permute-start(f32[384,768]{1,0:T(8,128)} %get-tuple-element.187.refs_0_), channel_id=1, source_target_pairs={{0,1},{1,0},{2,3},{3,2},{4,5},{5,4},{6,7},{7,6},{8,9},{9,8},{10,11... | collective-permute-start | bytes 3538952 | tf_op jit(solution)/shard_map/ppermute | solution.py:555
  299.4 51.1 %collective-permute-start.24 = (f32[384,768]{1,0:T(8,128)}, f32[384,768]{1,0:T(8,128)S(1)}, u32[]{:S(2)}, u32[]{:S(2)}) collective-permute-start(f32[384,768]{1,0:T(8,128)} %get-tuple-element.202.refs_2_), channel_id=1, source_target_pairs={{0,1},{1,0},{2,3},{3,2},{4,5},{5,4},{6,7},{7,6},{8,9},{9,8},{10,11... | collective-permute-start | bytes 3538952 | tf_op jit(solution)/shard_map/ppermute | solution.py:555
  328.4 15.6 %collective-permute-start.18 = (f32[192,768]{1,0:T(8,128)}, f32[192,768]{1,0:T(8,128)}, u32[]{:S(2)}, u32[]{:S(2)}) collective-permute-start(f32[192,768]{1,0:T(8,128)} %get-tuple-element.239.a), channel_id=1, source_target_pairs={{0,2},{1,3},{2,0},{3,1},{4,6},{5,7},{6,4},{7,5},{8,10},{9,11},{10,... | collective-permute-start | bytes 1769480 | tf_op jit(solution)/shard_map/ppermute | solution.py:555
  329.9 15.3 %collective-permute-start.19 = (f32[192,768]{1,0:T(8,128)}, f32[192,768]{1,0:T(8,128)}, u32[]{:S(2)}, u32[]{:S(2)}) collective-permute-start(f32[192,768]{1,0:T(8,128)} %get-tuple-element.240.c), channel_id=1, source_target_pairs={{0,16},{16,0},{1,17},{17,1},{2,18},{18,2},{3,19},{19,3},{4,20},{20... | collective-permute-start | bytes 1769480 | tf_op jit(solution)/shard_map/ppermute | solution.py:555
  344.0 7.0 %collective-permute-start.23 = (f32[384,768]{1,0:T(8,128)}, f32[384,768]{1,0:T(8,128)}, u32[]{:S(2)}, u32[]{:S(2)}) collective-permute-start(f32[384,768]{1,0:T(8,128)} %collective-permute-done.20.refs_1_), channel_id=1, source_target_pairs={{0,1},{1,0},{2,3},{3,2},{4,5},{5,4},{6,7},{7,6},{8,9},{9,8},{10,11... | collective-permute-start | bytes 3538952 | tf_op jit(solution)/shard_map/ppermute | solution.py:555
  348.4 27.4 %collective-permute-start.26 = (f32[384,768]{1,0:T(8,128)}, f32[384,768]{1,0:T(8,128)S(1)}, u32[]{:S(2)}, u32[]{:S(2)}) collective-permute-start(f32[384,768]{1,0:T(8,128)} %get-tuple-element.200.refs_0_), channel_id=1, source_target_pairs={{0,16},{16,0},{1,17},{17,1},{2,18},{18,2},{3,19},{19,3},{4,20},{20... | collective-permute-start | bytes 3538952 | tf_op jit(solution)/shard_map/ppermute | solution.py:555
  349.8 27.2 %collective-permute-start.27 = (f32[384,768]{1,0:T(8,128)}, f32[384,768]{1,0:T(8,128)}, u32[]{:S(2)}, u32[]{:S(2)}) collective-permute-start(f32[384,768]{1,0:T(8,128)} %get-tuple-element.208.refs_2_), channel_id=1, source_target_pairs={{0,2},{1,3},{2,0},{3,1},{4,6},{5,7},{6,4},{7,5},{8,10},{9,11},{10,... | collective-permute-start | bytes 3538952 | tf_op jit(solution)/shard_map/ppermute | solution.py:555
  350.4 71.9 %copy-start.7 = (f32[384,768]{1,0:T(8,128)}, f32[384,768]{1,0:T(8,128)S(1)}, u32[]{:S(2)}) copy-start(f32[384,768]{1,0:T(8,128)S(1)} %collective-permute-done.22.refs_0_) | copy-start | bytes 3538948
  350.4 26.6 %collective-permute-start.25 = (f32[384,768]{1,0:T(8,128)}, f32[384,768]{1,0:T(8,128)}, u32[]{:S(2)}, u32[]{:S(2)}) collective-permute-start(f32[384,768]{1,0:T(8,128)} %collective-permute-done.21.refs_3_), channel_id=1, source_target_pairs={{0,1},{1,0},{2,3},{3,2},{4,5},{5,4},{6,7},{7,6},{8,9},{9,8},{10,11... | collective-permute-start | bytes 3538952 | tf_op jit(solution)/shard_map/ppermute | solution.py:555
  350.5 71.8 %copy-start.8 = (f32[384,768]{1,0:T(8,128)}, f32[384,768]{1,0:T(8,128)S(1)}, u32[]{:S(2)}) copy-start(f32[384,768]{1,0:T(8,128)S(1)} %collective-permute-done.24.refs_2_) | copy-start | bytes 3538948
  350.5 64.4 %collective-permute-start.28 = (f32[384,768]{1,0:T(8,128)}, f32[384,768]{1,0:T(8,128)}, u32[]{:S(2)}, u32[]{:S(2)}) collective-permute-start(f32[384,768]{1,0:T(8,128)} %get-tuple-element.200.refs_0_), channel_id=1, source_target_pairs={{0,1},{1,0},{2,3},{3,2},{4,5},{5,4},{6,7},{7,6},{8,9},{9,8},{10,11... | collective-permute-start | bytes 3538952 | tf_op jit(solution)/shard_map/ppermute | solution.py:555
  351.0 81.9 %collective-permute-start.30 = (f32[384,768]{1,0:T(8,128)}, f32[384,768]{1,0:T(8,128)}, u32[]{:S(2)}, u32[]{:S(2)}) collective-permute-start(f32[384,768]{1,0:T(8,128)} %get-tuple-element.208.refs_2_), channel_id=1, source_target_pairs={{0,1},{1,0},{2,3},{3,2},{4,5},{5,4},{6,7},{7,6},{8,9},{9,8},{10,11... | collective-permute-start | bytes 3538952 | tf_op jit(solution)/shard_map/ppermute | solution.py:555
  375.8 46.5 %copy-start.9 = (f32[384,768]{1,0:T(8,128)}, f32[384,768]{1,0:T(8,128)S(1)}, u32[]{:S(2)}) copy-start(f32[384,768]{1,0:T(8,128)S(1)} %collective-permute-done.26.refs_1_) | copy-start | bytes 3538948
  375.8 57.1 %collective-permute-start.29 = (f32[384,768]{1,0:T(8,128)S(1)}, f32[384,768]{1,0:T(8,128)}, u32[]{:S(2)}, u32[]{:S(2)}) collective-permute-start(f32[384,768]{1,0:T(8,128)S(1)} %collective-permute-done.26.refs_1_), channel_id=1, source_target_pairs={{0,1},{1,0},{2,3},{3,2},{4,5},{5,4},{6,7},{7,6},{8,9},{9,8},{10,11... | collective-permute-start | bytes 3538952 | tf_op jit(solution)/shard_map/ppermute | solution.py:555
  377.0 55.9 %collective-permute-start.31 = (f32[384,768]{1,0:T(8,128)}, f32[384,768]{1,0:T(8,128)}, u32[]{:S(2)}, u32[]{:S(2)}) collective-permute-start(f32[384,768]{1,0:T(8,128)} %collective-permute-done.27.refs_3_), channel_id=1, source_target_pairs={{0,1},{1,0},{2,3},{3,2},{4,5},{5,4},{6,7},{7,6},{8,9},{9,8},{10,11... | collective-permute-start | bytes 3538952 | tf_op jit(solution)/shard_map/ppermute | solution.py:555
  413.4 24.8 %collective-permute-start.32 = (f32[256,768]{1,0:T(8,128)}, f32[256,768]{1,0:T(8,128)}, u32[]{:S(2)}, u32[]{:S(2)}) collective-permute-start(f32[256,768]{1,0:T(8,128)} %get-tuple-element.241.a), channel_id=1, source_target_pairs={{0,2},{1,3},{2,0},{3,1},{4,6},{5,7},{6,4},{7,5},{8,10},{9,11},{10,... | collective-permute-start | bytes 2359304 | tf_op jit(solution)/shard_map/ppermute | solution.py:555
  414.9 23.3 %collective-permute-start.33 = (f32[208,768]{1,0:T(8,128)}, f32[208,768]{1,0:T(8,128)}, u32[]{:S(2)}, u32[]{:S(2)}) collective-permute-start(f32[208,768]{1,0:T(8,128)} %get-tuple-element.242.c), channel_id=1, source_target_pairs={{0,16},{16,0},{1,17},{17,1},{2,18},{18,2},{3,19},{19,3},{4,20},{20... | collective-permute-start | bytes 1916936 | tf_op jit(solution)/shard_map/ppermute | solution.py:555
  441.7 35.7 %collective-permute-start.34 = (f32[512,768]{1,0:T(8,128)}, f32[512,768]{1,0:T(8,128)}, u32[]{:S(2)}, u32[]{:S(2)}) collective-permute-start(f32[512,768]{1,0:T(8,128)} %get-tuple-element.216.refs_0_), channel_id=1, source_target_pairs={{0,16},{16,0},{1,17},{17,1},{2,18},{18,2},{3,19},{19,3},{4,20},{20... | collective-permute-start | bytes 4718600 | tf_op jit(solution)/shard_map/ppermute | solution.py:555
  442.3 35.6 %collective-permute-start.35 = (f32[416,768]{1,0:T(8,128)}, f32[416,768]{1,0:T(8,128)}, u32[]{:S(2)}, u32[]{:S(2)}) collective-permute-start(f32[416,768]{1,0:T(8,128)} %get-tuple-element.218.refs_2_), channel_id=1, source_target_pairs={{0,2},{1,3},{2,0},{3,1},{4,6},{5,7},{6,4},{7,5},{8,10},{9,11},{10,... | collective-permute-start | bytes 3833864 | tf_op jit(solution)/shard_map/ppermute | solution.py:555
  442.8 41.0 %collective-permute-start.36 = (f32[512,768]{1,0:T(8,128)}, f32[512,768]{1,0:T(8,128)S(1)}, u32[]{:S(2)}, u32[]{:S(2)}) collective-permute-start(f32[512,768]{1,0:T(8,128)} %get-tuple-element.216.refs_0_), channel_id=1, source_target_pairs={{0,1},{1,0},{2,3},{3,2},{4,5},{5,4},{6,7},{7,6},{8,9},{9,8},{10,11... | collective-permute-start | bytes 4718600 | tf_op jit(solution)/shard_map/ppermute | solution.py:555
  477.4 7.4 %collective-permute-start.37 = (f32[512,768]{1,0:T(8,128)}, f32[512,768]{1,0:T(8,128)S(1)}, u32[]{:S(2)}, u32[]{:S(2)}) collective-permute-start(f32[512,768]{1,0:T(8,128)} %collective-permute-done.34.refs_1_), channel_id=1, source_target_pairs={{0,1},{1,0},{2,3},{3,2},{4,5},{5,4},{6,7},{7,6},{8,9},{9,8},{10,11... | collective-permute-start | bytes 4718600 | tf_op jit(solution)/shard_map/ppermute | solution.py:555
  477.4 6.4 %collective-permute-start.38 = (f32[416,768]{1,0:T(8,128)}, f32[416,768]{1,0:T(8,128)}, u32[]{:S(2)}, u32[]{:S(2)}) collective-permute-start(f32[416,768]{1,0:T(8,128)} %get-tuple-element.218.refs_2_), channel_id=1, source_target_pairs={{0,1},{1,0},{2,3},{3,2},{4,5},{5,4},{6,7},{7,6},{8,9},{9,8},{10,11... | collective-permute-start | bytes 3833864 | tf_op jit(solution)/shard_map/ppermute | solution.py:555
  477.9 6.9 %collective-permute-start.39 = (f32[416,768]{1,0:T(8,128)}, f32[416,768]{1,0:T(8,128)}, u32[]{:S(2)}, u32[]{:S(2)}) collective-permute-start(f32[416,768]{1,0:T(8,128)} %collective-permute-done.35.refs_3_), channel_id=1, source_target_pairs={{0,1},{1,0},{2,3},{3,2},{4,5},{5,4},{6,7},{7,6},{8,9},{9,8},{10,11... | collective-permute-start | bytes 3833864 | tf_op jit(solution)/shard_map/ppermute | solution.py:555
  (9 other events, 10.7 us)
Sparse Core Ops, SparseCore 0:
  164.8 56.6 all-reduce.6
  271.0 57.4 all-reduce.8
  350.5 62.8 all-reduce.10
